TPU v7x, 32 devices: a whole 2x2x4 slice. The times are simulated.
32 devices in a mesh: seq: 4 (over z), dp: 8 (over y, x, core).
Axes of the slice: x: 2, y: 2, z: 4, core: 2. Of those that a mesh axis runs over, the one named last changes fastest.
Arguments:
- layer_in: bfloat16 [2, 8, 1024, 768], P(None, 'dp', 'seq'), may hold values from -6 to 6
- cotangent: bfloat16 [2, 8, 1024, 768], P(None, 'dp', 'seq'), may hold values from -6 to 6
- valid_len: int32 [2, 8], P(None, 'dp'), may hold values from 512 to 1024, as said below
- sep_pos: int32 [2, 8], P(None, 'dp'), may hold values from 128 to 768, as said below
- w_query: bfloat16 [768, 384], P(('seq', 'dp')), may hold values from -0.21875 to 0.21875
- w_key: bfloat16 [768, 384], P(('seq', 'dp')), may hold values from -0.21875 to 0.21875
- w_value: bfloat16 [768, 384], P(('seq', 'dp')), may hold values from -0.21875 to 0.21875
- w_depth: bfloat16 [9, 768], P(None, ('seq', 'dp')), may hold values from -2 to 2
- w_point: bfloat16 [768, 384], P(('seq', 'dp')), may hold values from -0.21875 to 0.21875
- w_kernel: bfloat16 [20736], P(('seq', 'dp')), may hold values from -0.3125 to 0.3125
- w_convout: bfloat16 [768, 384], P(('seq', 'dp')), may hold values from -0.21875 to 0.21875
- w_output: bfloat16 [768, 768], P(('seq', 'dp')), may hold values from -0.875 to 0.875
- gain_attn: bfloat16 [768], P(('seq', 'dp')), may hold values from 0.3984375 to 1.59375
- shift_attn: bfloat16 [768], P(('seq', 'dp')), may hold values from -0.3984375 to 0.3984375
- w_up: bfloat16 [2, 384, 1536], P(None, None, ('seq', 'dp')), may hold values from -0.3125 to 0.3125
- w_down: bfloat16 [2, 1536, 384], P(None, ('seq', 'dp')), may hold values from -0.15625 to 0.15625
- gain_out: bfloat16 [768], P(('seq', 'dp')), may hold values from 0.3984375 to 1.59375
- shift_out: bfloat16 [768], P(('seq', 'dp')), may hold values from -0.3984375 to 0.3984375
Outputs:
- layer_out: bfloat16 [2, 8, 1024, 768], P(None, 'dp', 'seq')
- x_grad: float32 [2, 8, 1024, 768], P(None, 'dp', 'seq')
- grad_query: float32 [768, 384], P(('seq', 'dp'))
- grad_key: float32 [768, 384], P(('seq', 'dp'))
- grad_value: float32 [768, 384], P(('seq', 'dp'))
- grad_depth: float32 [9, 768], P(None, ('seq', 'dp'))
- grad_point: float32 [768, 384], P(('seq', 'dp'))
- grad_kernel: float32 [20736], P(('seq', 'dp'))
- grad_convout: float32 [768, 384], P(('seq', 'dp'))
- grad_output: float32 [768, 768], P(('seq', 'dp'))
- grad_gain_attn: float32 [768], P(('seq', 'dp'))
- grad_shift_attn: float32 [768], P(('seq', 'dp'))
- grad_up: float32 [2, 384, 1536], P(None, None, ('seq', 'dp'))
- grad_down: float32 [2, 1536, 384], P(None, ('seq', 'dp'))
- grad_gain_out: float32 [768], P(('seq', 'dp'))
- grad_shift_out: float32 [768], P(('seq', 'dp'))
Inputs may be any that keep to these rules, and one draw needn't show every extreme that they name: `valid_len`: for every index of dp, one of its rows over the 2 micro-batches, which one drawn from the seed, has all 1024 tokens. `sep_pos`: below the row's valid_len and at least valid_len // 4 (a quarter, rounded down).
All inputs are finite; a program needn't handle non-finite values.
Results may differ from a plain program's by a relative error of at most 0.015.
Values may be sent and summed in bfloat16 or wider, within the bound.
No kernel may reach another device: no remote copies, remote signals or barrier semaphores. Data moves between devices by JAX's collectives and lax.ppermute only.
A program may use at most 192 MiB of HBM per device.

v0:
```python
import functools

import jax
import jax.numpy as jnp
import numpy as np
from jax import lax
from jax.experimental import pallas as pl
from jax.experimental.pallas import tpu as pltpu
from jax.sharding import PartitionSpec as P

HEADS = 6
HEAD_DIM = 64
KERNEL = 9
GROUPS = 2
LEN = 1024
HALF = LEN // 2
WIDTH = 768
WIDE = HEADS * HEAD_DIM
CHUNK = 128
EDGE = 16
WINDOW = HALF + 2 * EDGE
BLOCKS = 32
HIDDEN = 48
PACK = 240
COST = 10**8

F32 = jnp.float32
BF16 = jnp.bfloat16

inv_root_two = 0.7071067811865476
inv_root_tau = 0.3989422804014327


def nn(a, b):
    return jnp.dot(a, b, preferred_element_type=F32)


def nt(a, b):
    return lax.dot_general(a, b, (((1,), (1,)), ((), ())), preferred_element_type=F32)


def tn(a, b):
    return lax.dot_general(a, b, (((0,), (0,)), ((), ())), preferred_element_type=F32)


def call(kernel, out_shape, args, scalars=1, scratch=(), micros=0):
    vmem = pl.BlockSpec(memory_space=pltpu.VMEM)
    smem = pl.BlockSpec(memory_space=pltpu.SMEM)
    return pl.pallas_call(
        kernel,
        out_shape=out_shape,
        in_specs=[smem] * scalars
        + [vmem] * (len(args) - scalars),
        out_specs=jax.tree.map(
            lambda s: smem if s.dtype == jnp.int32 else vmem, out_shape
        ),
        scratch_shapes=list(scratch),
        compiler_params=pltpu.CompilerParams(vmem_limit_bytes=56 * 1024 * 1024),
        cost_estimate=pl.CostEstimate(flops=micros * COST, bytes_accessed=0, transcendentals=0),
    )(*args)


def shape(dims, dtype):
    return jax.ShapeDtypeStruct(dims, dtype)


def lane(rows):
    return lax.broadcasted_iota(jnp.int32, (rows, CHUNK), 1)


def load_window(core, source, target, chunks):
    value = source(pl.ds(pl.multiple_of(core * (HALF - EDGE), EDGE), HALF + EDGE))
    start = pl.multiple_of(EDGE - core * EDGE, EDGE)
    edge = pl.multiple_of(core * (HALF + EDGE), EDGE)
    for c in range(chunks):
        target[c, pl.ds(edge, EDGE), :] = jnp.zeros((EDGE, CHUNK), F32)
        target[c, pl.ds(start, HALF + EDGE), :] = value[:, c * CHUNK : (c + 1) * CHUNK].astype(F32)


def weight(own, other, index):
    rows = slice(index * WIDE, (index + 1) * WIDE)
    return own[rows, :], other[rows, :]


def project(tokens, own, other, index):
    first, second = weight(own, other, index)
    return nn(tokens[:, :WIDE], first) + nn(tokens[:, WIDE:], second)


def fill_masks(info, masks):
    sep, valid, core = info[1], info[0], info[2]

    def segment(position):
        return jnp.where(position < sep, 0, jnp.where(position < valid, 1, 2))

    row = core * HALF + lax.broadcasted_iota(jnp.int32, (HALF, CHUNK), 0)
    own = segment(row)
    for j in range(KERNEL):
        masks[j] = (segment(row + (j - 4)) == own).astype(F32)


def prepare_kernel(info, tokens, *refs):
    weights, small, early, token_a, token_b = refs[:5], refs[5], refs[6], refs[7], refs[8]
    rows = weights[0].shape[0]
    odd = info[0]
    token_a[...] = tokens[pl.ds(odd, 1), 0][0]
    token_b[...] = tokens[pl.ds(1 - odd, 1), 0][0]
    pieces = [ref[...].astype(F32) for ref in weights] + [small[...].astype(F32)]
    for i in range(3):
        pair = jnp.concatenate(pieces[2 * i : 2 * i + 2], 0)
        early[2 * i * rows : 2 * i * rows + pair.shape[0], :] = pair.astype(BF16)


def permute_kernel(
    place, mine, theirs, own_a, own_b, other_a, other_b, codes, info, out, own_out, matrix
):
    z, core, me, rows = place[0], place[1], place[2], place[3]
    high = z >> 1
    for i in range(2):
        own_value = jnp.where(high == 0, mine[i, 0], mine[i, 1])
        other_value = jnp.where(high == 0, theirs[i, 0], theirs[i, 1])
        info[i] = jnp.where((z & 1) == core, own_value, other_value).astype(jnp.int32)
    info[2] = core
    info[3] = high
    features = (codes[0:1, :] ^ me) * rows + codes[1:2, :]
    matrix[...] = (
        (lax.broadcasted_iota(jnp.int32, (WIDTH, WIDTH), 0) == features)
        .astype(F32)
        .astype(BF16)
    )
    quarter = HALF // 2
    for side, pieces in ((core, (own_a, own_b)), (1 - core, (other_a, other_b))):
        for place, piece in zip((high, 1 - high), pieces):
            at = pl.multiple_of(side * HALF + place * quarter, quarter)
            out[pl.ds(at, quarter), :] = nn(piece[...], matrix[...]).astype(BF16)
    own_out[pl.ds(pl.multiple_of(high * quarter, quarter), quarter), :] = own_a[...]
    own_out[pl.ds(pl.multiple_of((1 - high) * quarter, quarter), quarter), :] = own_b[...]


def attend_kernel(info, tokens, *refs):
    parts, refs = refs[:-8], refs[-8:]
    own, other, small_out, q_out, k_out, v_out, att_out, stat_out = refs
    core, valid = info[2], info[0]
    count = len(parts) // 2
    unit = WIDE // count
    rest = parts[0].shape[0] - 5 * unit
    for h, target in enumerate((own, other)):
        for i in range(count):
            part = parts[h * count + i]
            for w in range(5):
                target[w * WIDE + i * unit : w * WIDE + (i + 1) * unit, :] = part[
                    w * unit : (w + 1) * unit, :
                ]
            first = (h * count + i) * rest
            small_out[first : first + rest, :] = part[5 * unit :, :]
    mine = tokens[pl.ds(pl.multiple_of(core * HALF, HALF), HALF), :]
    q_out[...] = project(mine, own, other, 0).astype(BF16)
    k_out[...] = project(tokens[...], own, other, 1).astype(BF16)
    v_out[...] = project(tokens[...], own, other, 2).astype(BF16)
    rows = 256
    bias = jnp.where(
        lax.broadcasted_iota(jnp.int32, (1, LEN), 1) < valid, 0.0, -1e30
    ).astype(F32)
    for block in range(HALF // rows):
        at = slice(block * rows, (block + 1) * rows)
        stats = jnp.zeros((rows, CHUNK), F32)
        for pair in range(HEADS // 2):
            cols = slice(pair * CHUNK, (pair + 1) * CHUNK)
            q = q_out[at, cols] * BF16(0.125)
            k, v = k_out[:, cols], v_out[:, cols]
            results = []
            for head in range(2):
                keep = (lane(rows) < HEAD_DIM) == (head == 0)
                scores = nt(jnp.where(keep, q, BF16(0)), k) + bias
                peak = jnp.max(scores, -1, keepdims=True)
                exponent = jnp.exp(scores - peak)
                total = jnp.sum(exponent, -1, keepdims=True)
                results.append(nn(exponent.astype(BF16), v) / total)
                stats = jnp.where(
                    lane(rows) == 2 * pair + head, peak + jnp.log(total), stats
                )
            att_out[at, cols] = jnp.where(lane(rows) < HEAD_DIM, *results).astype(BF16)
        stat_out[at, :] = stats


def spread(j):
    row = lax.broadcasted_iota(jnp.int32, (CHUNK, WIDE), 0)
    col = lax.broadcasted_iota(jnp.int32, (CHUNK, WIDE), 1)
    return (row == (col >> 6) * KERNEL + j).astype(F32).astype(BF16)


def conv_kernel(
    info,
    tokens,
    own,
    other,
    q,
    att,
    taps_weight,
    depth_weight,
    context,
    key_out,
    attn_out,
    depth_out,
    values_out,
    window,
    logits,
    masks,
):
    core = info[2]
    load_window(core, lambda rows: tokens[rows, :], window, WIDTH // CHUNK)
    fill_masks(info, masks)
    rows = 64
    for c in range(WIDTH // CHUNK):
        cols = slice(c * CHUNK, (c + 1) * CHUNK)
        for b in range(HALF // rows):
            total = jnp.zeros((rows, CHUNK), F32)
            for j in range(KERNEL):
                first = EDGE - 4 + b * rows + j
                total = total + depth_weight[j : j + 1, cols] * window[c, first : first + rows, :]
            depth_out[b * rows : (b + 1) * rows, cols] = total.astype(BF16)
    key_conv = project(depth_out[...], own, other, 3)
    key_out[...] = key_conv
    attn_out[...] = (key_conv * q[...].astype(F32)).astype(BF16)
    load_window(
        core, lambda rows: project(tokens[rows, :], own, other, 4), values_out, WIDE // CHUNK
    )
    for j in range(KERNEL):
        logits[j] = nn(attn_out[...], nn(taps_weight[...], spread(j)).astype(BF16))
    context[:, :WIDE] = att[...]
    for b in range(HALF // rows):
        at = slice(b * rows, (b + 1) * rows)
        for c in range(WIDE // CHUNK):
            cols = slice(c * CHUNK, (c + 1) * CHUNK)
            peak = logits[0, at, cols]
            for j in range(1, KERNEL):
                peak = jnp.maximum(peak, logits[j, at, cols])
            total = jnp.zeros((rows, CHUNK), F32)
            result = jnp.zeros((rows, CHUNK), F32)
            for j in range(KERNEL):
                first = EDGE - 4 + b * rows + j
                exponent = jnp.exp(logits[j, at, cols] - peak)
                total = total + exponent
                result = result + exponent * masks[j, at, :] * values_out[
                    c, first : first + rows, :
                ]
            context[at, WIDE + c * CHUNK : WIDE + (c + 1) * CHUNK] = (result / total).astype(BF16)


def normalize(value):
    centred = value - jnp.mean(value, -1, keepdims=True)
    inv = lax.rsqrt(jnp.mean(centred * centred, -1, keepdims=True) + 1e-06)
    return centred * inv, inv


def normalize_back(grad, normed, inv, gain):
    e = grad * gain
    return inv * (
        e - jnp.mean(e, -1, keepdims=True) - normed * jnp.mean(e * normed, -1, keepdims=True)
    )


def piece_rows(info, step, rows):
    half = info[3] if step < 2 else 1 - info[3]
    return pl.ds(pl.multiple_of(half * (HALF // 2) + step % 2 * rows, rows), rows)


def sum_kernel(cut, kept, arrived, first_0, first_1, second_0, second_1):
    count = kept.shape[0] // 4
    for i in range(kept.shape[0]):
        total = kept[i].astype(F32) + arrived[i].astype(F32)
        high, low = i // (2 * count), i // count % 2
        (first_0, first_1)[high][i % (2 * count)] = total[:cut].astype(BF16)
        (second_0, second_1)[low][high * count + i % count] = total[cut:].astype(BF16)


def place_kernel(info, first, second, out):
    odd = info[0]
    out[pl.ds(odd, 1), 0] = first[...].astype(out.dtype)[None]
    out[pl.ds(1 - odd, 1), 0] = second[...].astype(out.dtype)[None]


def feed_kernel(
    info,
    order,
    context,
    tokens,
    late,
    cot_a,
    cot_b,
    gains,
    matrix,
    layer_a,
    layer_b,
    first_out,
    context_grad,
    kept,
    sent,
    small_out,
    out_weight,
    up,
    down,
    act,
    slope,
    normed,
    attn,
    attn_low,
    grad_low,
    branch_low,
    second,
    scale,
):
    rows = 128
    steps = [slice(i * rows, (i + 1) * rows) for i in range(HALF // rows)]
    gain_attn, shift_attn = gains[0:1, :], gains[1:2, :]
    gain_out, shift_out = gains[2:3, :], gains[3:4, :]
    for i in range(BLOCKS // 2):
        sides = [late[2 * i + k, 0:HIDDEN, :].astype(F32) for k in range(2)]
        out_weight[i * HIDDEN : (i + 1) * HIDDEN, :] = jnp.concatenate(
            [jnp.concatenate([s[: HIDDEN // 2], s[HIDDEN // 2 :]], 1) for s in sides], 0
        ).astype(BF16)
    for h in range(2):
        for i in range(BLOCKS // 2):
            source = order[h * (BLOCKS // 2) + i]
            for g in range(GROUPS):
                at = slice(i * HIDDEN, (i + 1) * HIDDEN)
                up[g, h, at, :] = late[source, (1 + g) * HIDDEN : (2 + g) * HIDDEN, :]
                down[g, h, at, :] = late[source, (3 + g) * HIDDEN : (4 + g) * HIDDEN, :]
    for at in steps:
        branch = nn(context[at, :], out_weight[...]) + tokens[at, :].astype(F32)
        n, inv = normalize(branch)
        normed[at, :] = n
        scale[at, :] = inv
        value = n * gain_attn + shift_attn
        attn[at, :] = value
        attn_low[at, :] = value.astype(BF16)
    for g in range(GROUPS):
        part = slice(g * WIDE, (g + 1) * WIDE)
        for h in range(2):
            for at in steps:
                pre = nt(attn_low[at, part], up[g, h])
                cdf = 0.5 * (1.0 + lax.erf(pre * inv_root_two))
                act[g, h, at, :] = (pre * cdf).astype(BF16)
                slope[g, h, at, :] = cdf + pre * jnp.exp(-0.5 * pre * pre) * inv_root_tau
    gain_grad = jnp.zeros((1, WIDTH), F32)
    shift_grad = jnp.zeros((1, WIDTH), F32)
    for step in range(HALF // rows):
        piece, inner = step // 2, slice(step % 2 * rows, (step % 2 + 1) * rows)
        at = piece_rows(info, step, rows)
        value = attn[at, :] + jnp.concatenate(
            [
                nn(act[g, 0, at, :], down[g, 0]) + nn(act[g, 1, at, :], down[g, 1])
                for g in range(GROUPS)
            ],
            1,
        )
        n, inv = normalize(value)
        (layer_a, layer_b)[piece][inner, :] = (n * gain_out + shift_out).astype(BF16)
        grad = (cot_a, cot_b)[piece][inner, :].astype(F32)
        gain_grad = gain_grad + jnp.sum(grad * n, 0, keepdims=True)
        shift_grad = shift_grad + jnp.sum(grad, 0, keepdims=True)
        value = normalize_back(grad, n, inv, gain_out)
        second[at, :] = value
        grad_low[at, :] = value.astype(BF16)
    small_out[2:3, :] = gain_grad
    small_out[3:4, :] = shift_grad
    for g in range(GROUPS):
        part = slice(g * WIDE, (g + 1) * WIDE)
        for h in range(2):
            target = (kept, sent)[h]
            result = tn(act[g, h], grad_low[:, part]).astype(BF16)
            for i in range(BLOCKS // 2):
                target[i, (3 + g) * HIDDEN : (4 + g) * HIDDEN, :] = result[
                    i * HIDDEN : (i + 1) * HIDDEN
                ]
            for at in steps:
                act[g, h, at, :] = (
                    nt(grad_low[at, part], down[g, h]) * slope[g, h, at, :]
                ).astype(BF16)
            result = tn(act[g, h], attn_low[:, part]).astype(BF16)
            for i in range(BLOCKS // 2):
                target[i, (1 + g) * HIDDEN : (2 + g) * HIDDEN, :] = result[
                    i * HIDDEN : (i + 1) * HIDDEN
                ]
    gain_grad = jnp.zeros((1, WIDTH), F32)
    shift_grad = jnp.zeros((1, WIDTH), F32)
    for at in steps:
        grad = second[at, :] + jnp.concatenate(
            [nn(act[g, 0, at, :], up[g, 0]) + nn(act[g, 1, at, :], up[g, 1]) for g in range(GROUPS)],
            1,
        )
        n = normed[at, :]
        gain_grad = gain_grad + jnp.sum(grad * n, 0, keepdims=True)
        shift_grad = shift_grad + jnp.sum(grad, 0, keepdims=True)
        value = normalize_back(grad, n, scale[at, :], gain_attn)
        first_out[at, :] = value
        branch_low[at, :] = value.astype(BF16)
        context_grad[at, :] = nt(branch_low[at, :], out_weight[...]).astype(BF16)
        grad_low[at, :] = nn(context[at, :], matrix[...]).astype(BF16)
    small_out[0:1, :] = gain_grad
    small_out[1:2, :] = shift_grad
    small_out[4:8, :] = jnp.zeros((4, WIDTH), F32)
    for h in range(2):
        result = tn(grad_low[:, h * WIDE : (h + 1) * WIDE], branch_low[...])
        for i in range(BLOCKS // 2):
            piece = result[i * (HIDDEN // 2) : (i + 1) * (HIDDEN // 2)]
            (kept, sent)[h][i, 0:HIDDEN, :] = jnp.concatenate(
                [piece[:, :WIDE], piece[:, WIDE:]], 0
            ).astype(BF16)


def shifted_sum(source, step, scale=None):
    total = jnp.zeros((32, CHUNK), F32)
    for j in range(KERNEL):
        first = step + 4 - j
        low, high = max(first, 0), min(first + 32, WINDOW)
        piece = source(j)[low:high, :]
        if high - low < 32:
            zero = jnp.zeros((32 - (high - low), CHUNK), F32)
            piece = jnp.concatenate([zero, piece] if low > first else [piece, zero], 0)
        total = total + (piece if scale is None else scale(j) * piece)
    return total


def taps_back_kernel(
    info,
    q,
    context_grad,
    key_conv,
    conv_attn,
    values,
    taps_weight,
    query_out,
    key_low,
    kernel_out,
    values_grad,
    rim_out,
    logits,
    masks,
    sums,
    pads,
    compact,
):
    core = info[2]
    fill_masks(info, masks)
    rows = 64
    steps = [slice(i * rows, (i + 1) * rows) for i in range(HALF // rows)]
    block = (lax.broadcasted_iota(jnp.int32, (CHUNK, CHUNK), 0) >> 6) == (
        lax.broadcasted_iota(jnp.int32, (CHUNK, CHUNK), 1) >> 6
    )
    ones = block.astype(F32).astype(BF16)
    pick_row = lax.broadcasted_iota(jnp.int32, (CHUNK, CHUNK), 0)
    pick_col = lax.broadcasted_iota(jnp.int32, (CHUNK, CHUNK), 1)
    for j in range(KERNEL):
        logits[j] = nn(conv_attn[...], nn(taps_weight[...], spread(j)).astype(BF16))
        pads[j, 0:EDGE, :] = jnp.zeros((EDGE, CHUNK), F32)
        pads[j, HALF + EDGE : WINDOW, :] = jnp.zeros((EDGE, CHUNK), F32)
    total_compact = jnp.zeros((HALF, CHUNK), F32)
    for c in range(WIDE // CHUNK):
        cols = slice(c * CHUNK, (c + 1) * CHUNK)
        grad_cols = slice(WIDE + c * CHUNK, WIDE + (c + 1) * CHUNK)
        for j in range(KERNEL):
            product = (
                context_grad[:, grad_cols].astype(F32)
                * values[c, EDGE - 4 + j : EDGE - 4 + j + HALF, :]
            )
            sums[j] = nn(product.astype(BF16), ones)
        for b, at in enumerate(steps):
            grad = context_grad[at, grad_cols].astype(F32)
            peak = logits[0, at, cols]
            for j in range(1, KERNEL):
                peak = jnp.maximum(peak, logits[j, at, cols])
            total = jnp.zeros((rows, CHUNK), F32)
            dot = jnp.zeros((rows, CHUNK), F32)
            for j in range(KERNEL):
                exponent = jnp.exp(logits[j, at, cols] - peak)
                mask = masks[j, at, :]
                logits[j, at, cols] = exponent
                change = sums[j, at, :] * mask
                sums[j, at, :] = change
                total = total + exponent
                dot = dot + exponent * change
            inv = 1.0 / total
            dot = dot * inv
            inside = slice(EDGE + b * rows, EDGE + (b + 1) * rows)
            for j in range(KERNEL):
                tap = logits[j, at, cols] * inv
                pads[j, inside, :] = tap * masks[j, at, :] * grad
                compact[j, at, :] = (tap * (sums[j, at, :] - dot)).astype(BF16)
        for j in range(KERNEL):
            pick = (pick_row & 63 == 0) & (pick_col == (2 * c + (pick_row >> 6)) * KERNEL + j)
            total_compact = total_compact + nn(compact[j], pick.astype(F32).astype(BF16))
        for b in range(WINDOW // 32):
            values_grad[c, b * 32 : (b + 1) * 32, :] = shifted_sum(lambda j: pads.at[j], b * 32)
    compact_low = total_compact.astype(BF16)
    kernel_out[...] = tn(conv_attn[...], compact_low)
    attn_grad = nt(compact_low, taps_weight[...])
    query_out[...] = attn_grad * key_conv[...]
    key_low[...] = (attn_grad * q[...].astype(F32)).astype(BF16)
    rim = pl.multiple_of((1 - core) * (HALF + EDGE), EDGE)
    for c in range(WIDE // CHUNK):
        rim_out[:, c * CHUNK : (c + 1) * CHUNK] = values_grad[c, pl.ds(rim, EDGE), :].astype(BF16)


def depth_back_kernel(
    info,
    tokens,
    own,
    other,
    key_low,
    depth_low,
    depth_weight,
    point_out,
    depth_grad,
    back_out,
    rim_out,
    window,
):
    core = info[2]
    load_window(core, lambda rows: tokens[rows, :], window, WIDTH // CHUNK)
    point_out[...] = tn(depth_low[...], key_low[...]).astype(BF16)
    depth_grad[...] = jnp.zeros((16, WIDTH), F32)
    for side, rows_weight in enumerate(weight(own, other, 3)):
        back = nt(key_low[...], rows_weight)
        for k in range(WIDE // CHUNK):
            c = side * (WIDE // CHUNK) + k
            back_out[c, 0:EDGE, :] = jnp.zeros((EDGE, CHUNK), F32)
            back_out[c, HALF + EDGE : WINDOW, :] = jnp.zeros((EDGE, CHUNK), F32)
            back_out[c, EDGE : HALF + EDGE, :] = back[:, k * CHUNK : (k + 1) * CHUNK]
    for c in range(WIDTH // CHUNK):
        cols = slice(c * CHUNK, (c + 1) * CHUNK)
        totals = [jnp.zeros((8, CHUNK), F32) for _ in range(KERNEL)]
        for b in range(HALF // 32):
            grad = back_out[c, EDGE + b * 32 : EDGE + (b + 1) * 32, :]
            for j in range(KERNEL):
                first = EDGE - 4 + b * 32 + j
                product = grad * window[c, first : first + 32, :]
                totals[j] = totals[j] + (
                    (product[0:8] + product[8:16]) + (product[16:24] + product[24:32])
                )
        for j in range(KERNEL):
            depth_grad[j : j + 1, cols] = jnp.sum(totals[j], 0, keepdims=True)
        low, high = (
            shifted_sum(lambda j: back_out.at[c], step, lambda j: depth_weight[j : j + 1, cols])
            for step in (0, WINDOW - 32)
        )
        turned = (c + WIDE // CHUNK) % (WIDTH // CHUNK)
        rim_out[:, turned * CHUNK : (turned + 1) * CHUNK] = jnp.where(
            core == 0, high[32 - EDGE :], low[:EDGE]
        ).astype(BF16)


def attend_back_kernel(
    info, q, k, v, context, context_grad, stats, query_out, own_out, message, key_sum, value_sum
):
    core, valid = info[2], info[0]
    rows = 256
    live = lax.broadcasted_iota(jnp.int32, (LEN, CHUNK), 0) < valid
    for pair in range(HEADS // 2):
        cols = slice(pair * CHUNK, (pair + 1) * CHUNK)
        keys, vals = k[:, cols], v[:, cols]
        for head in range(2):
            even = head == 0
            base = HEAD_DIM if even else 0
            key_lane = lane(LEN)
            keep_key = (key_lane < HEAD_DIM) == even
            keys_more = jnp.where(
                keep_key,
                keys.astype(F32),
                jnp.where(
                    key_lane == base,
                    jnp.where(live, 0.0, -1e30),
                    jnp.where(key_lane < base + 4, 1.0, 0.0),
                ),
            ).astype(BF16)
            vals_more = jnp.where(
                keep_key, vals.astype(F32), jnp.where(key_lane < base + 3, 1.0, 0.0)
            ).astype(BF16)
            keys_turned = keys_more.T
            for block in range(HALF // rows):
                at = slice(block * rows, (block + 1) * rows)
                here = lane(rows)
                keep = (here < HEAD_DIM) == even

                def three(value):
                    high = value.astype(BF16).astype(F32)
                    middle = (value - high).astype(BF16).astype(F32)
                    return high, middle, value - high - middle

                grad = context_grad[at, cols].astype(F32)
                product = jnp.where(keep, grad * context[at, cols].astype(F32), 0.0)
                dots = three(-jnp.sum(product, -1, keepdims=True))
                stat = three(-stats[at, 2 * pair + head : 2 * pair + head + 1])
                grad_more = jnp.where(
                    keep,
                    grad,
                    jnp.where(
                        here == base,
                        dots[0],
                        jnp.where(
                            here == base + 1, dots[1], jnp.where(here == base + 2, dots[2], 0.0)
                        ),
                    ),
                ).astype(BF16)
                query_more = jnp.where(
                    keep,
                    q[at, cols].astype(F32) * 0.125,
                    jnp.where(
                        here == base,
                        1.0,
                        jnp.where(
                            here == base + 1,
                            stat[0],
                            jnp.where(
                                here == base + 2, stat[1], jnp.where(here == base + 3, stat[2], 0.0)
                            ),
                        ),
                    ),
                ).astype(BF16)
                probs = jnp.exp(nt(keys_more, query_more))
                change = (probs * nt(vals_more, grad_more)).astype(BF16)
                value_part = nn(probs.astype(BF16), grad_more)
                key_part = nn(change, query_more)
                query_part = nn(keys_turned, change).T * 0.125
                if block == 0:
                    value_total, key_total = value_part, key_part
                else:
                    value_total, key_total = value_total + value_part, key_total + key_part
                if even:
                    query_out[at, cols] = query_part
                else:
                    query_out[at, cols] = jnp.where(keep, query_part, query_out[at, cols])
            if even:
                key_sum[:, cols] = key_total
                value_sum[:, cols] = value_total
            else:
                key_sum[:, cols] = jnp.where(keep_key, key_total, key_sum[:, cols])
                value_sum[:, cols] = jnp.where(keep_key, value_total, value_sum[:, cols])
    mine = pl.ds(pl.multiple_of(core * HALF, HALF), HALF)
    theirs = pl.ds(pl.multiple_of((1 - core) * HALF, HALF), HALF)
    own_out[:, :WIDE] = key_sum[mine, :]
    own_out[:, WIDE:] = value_sum[mine, :]
    message[:, :WIDE] = key_sum[theirs, :].astype(BF16)
    message[:, WIDE:] = value_sum[theirs, :].astype(BF16)


def grads_kernel(
    info,
    tokens,
    query_attn,
    query_conv,
    own_part,
    arrived,
    rim_values,
    values_grad,
    point_grad,
    small,
    kept,
    sent,
    low_out,
    values_sum,
):
    core = info[2]
    rim = pl.ds(pl.multiple_of((1 - core) * (HALF - EDGE), EDGE), EDGE)
    for c in range(WIDE // CHUNK):
        cols = slice(c * CHUNK, (c + 1) * CHUNK)
        values_sum[:, cols] = values_grad[c, EDGE : EDGE + HALF, :]
    values_sum[rim, :] = values_sum[rim, :] + rim_values[...].astype(F32)
    both = own_part[...] + arrived[...].astype(F32)
    low_out[0] = (query_attn[...] + query_conv[...]).astype(BF16)
    low_out[1] = both[:, :WIDE].astype(BF16)
    low_out[2] = both[:, WIDE:].astype(BF16)
    low_out[3] = values_sum[...].astype(BF16)
    mine = pl.ds(pl.multiple_of(core * HALF, HALF), HALF)
    unit = HIDDEN // 2
    for h in range(2):
        part = tokens[mine, h * WIDE : (h + 1) * WIDE]
        results = [tn(part, low_out[n]) for n in range(4)]
        point = point_grad[h * WIDE : (h + 1) * WIDE, :].astype(F32)
        target = (kept, sent)[h]
        for i in range(BLOCKS // 2):
            at = slice(i * unit, (i + 1) * unit)
            target[i, 0:48, :] = jnp.concatenate([results[0][at], results[1][at]], 0).astype(BF16)
            target[i, 48:96, :] = jnp.concatenate([results[2][at], point[at]], 0).astype(BF16)
            target[i, 96:128, :] = jnp.concatenate(
                [results[3][at], small[h * (BLOCKS // 2) + i]], 0
            ).astype(BF16)


def inputs_kernel(
    info,
    own,
    other,
    matrix,
    depth_weight,
    low,
    rim_inputs,
    back,
    first_grad,
    x_a,
    x_b,
    inputs,
):
    core = info[2]
    rim = pl.ds(pl.multiple_of((1 - core) * (HALF - EDGE), EDGE), EDGE)
    for c in range(WIDTH // CHUNK):
        cols = slice(c * CHUNK, (c + 1) * CHUNK)
        for b in range(HALF // 32):
            inputs[b * 32 : (b + 1) * 32, cols] = shifted_sum(
                lambda j: back.at[c], EDGE + b * 32, lambda j: depth_weight[j : j + 1, cols]
            )
    inputs[rim, :] = inputs[rim, :] + rim_inputs[...].astype(F32)
    for h in range(2):
        rows = (own, other)[h]
        total = inputs[:, h * WIDE : (h + 1) * WIDE]
        for n, index in enumerate((0, 1, 2, 4)):
            total = total + nt(low[n], rows[index * WIDE : (index + 1) * WIDE, :])
        inputs[:, h * WIDE : (h + 1) * WIDE] = total
    for step in range(4):
        at = piece_rows(info, step, CHUNK)
        value = nt(inputs[at, :].astype(BF16), matrix[...]) + first_grad[at, :]
        inner = slice(step % 2 * CHUNK, (step % 2 + 1) * CHUNK)
        (x_a, x_b)[step // 2][inner, :] = value.astype(BF16)


def dp_groups(count):
    masks = []
    bit = 2
    while bit < count:
        if bit * 2 < count:
            masks.append((bit, 2 * bit, 3 * bit))
            bit *= 4
        else:
            masks.append((bit,))
            bit *= 2
    return masks


def swap(x, axis, mask):
    count = lax.axis_size(axis)
    return lax.ppermute(x, axis, [(i, i ^ mask) for i in range(count)])


def relative_codes():
    seq, dp = lax.axis_size("seq"), lax.axis_size("dp")
    codes = [j * dp for j in range(seq)]
    for masks in dp_groups(dp):
        codes = [c ^ m for m in (0,) + masks for c in codes]
    return codes + [c ^ 1 for c in codes]


def add_up(parts):
    total = parts[0].astype(jnp.float32)
    for part in parts[1:]:
        total = total + part.astype(jnp.float32)
    return total


def token_perms():
    seq, dp = lax.axis_size("seq"), lax.axis_size("dp")
    first, second = [], []
    for z in range(seq):
        for d in range(dp):
            core, rest = d & 1, d & ~1
            odd = z & 1
            first.append((z * dp + d, (2 * odd + core) * dp + rest + (z >> 1)))
            second.append((z * dp + d, (2 * (1 - odd) + core) * dp + rest + (z >> 1)))
    return first, second


def pad_rows(x, multiple):
    return jnp.pad(x, ((0, -x.shape[0] % multiple), (0, 0)))


def merge(packs, rows):
    cut = packs[0].shape[0] // (5 * rows + 8) * (5 * rows)
    weights = jnp.concatenate([p[:cut].reshape(5, -1, WIDE) for p in packs], 1)
    return jnp.concatenate([weights.reshape(-1, WIDE)] + [p[cut:] for p in packs])


def gather_weights(pack, rows, *tokens):
    held = merge([pack] + [swap(pack, "seq", j) for j in range(1, lax.axis_size("seq"))], rows)
    tokens = send_pieces(*tokens)
    groups = dp_groups(lax.axis_size("dp"))
    for masks in groups[:-1]:
        held = merge([held] + [swap(held, "dp", m) for m in masks], rows)
    return [held] + [swap(held, "dp", m) for m in groups[-1]], *tokens


def send_pieces(a, b, back=False):
    first, second = token_perms()
    if back:
        first, second = ([(t, s) for s, t in perm] for perm in (first, second))
    return lax.ppermute(a, ("seq", "dp"), first), lax.ppermute(b, ("seq", "dp"), second)


def to_pieces(x):
    odd = lax.axis_index("seq") & 1
    a, b = (lax.dynamic_index_in_dim(x, index, 0, False) for index in (odd, 1 - odd))
    return send_pieces(a, b)


def wait_for(arrays, value):
    return lax.optimization_barrier((arrays, value))


class Scatter:
    def __init__(self, kept, sent, cut):
        self.bits = lax.axis_size("dp").bit_length() - 2
        self.stage = 0
        self.cut = cut
        self.held = kept, sent

    def pieces(self, whole, rows):
        dims = (2,) * self.bits + (-1,) + whole[0].shape[1:]
        return [part.reshape(dims)[..., rows, :] for part in whole]

    def step(self, value):
        if self.stage == 0:
            kept, sent = self.held
            arrived, value = wait_for(swap(sent, "dp", 1), value)
            if self.bits == 2:
                self.stage = 1
                size, rows, wide = kept.shape
                halves = [
                    shape((size // 2, n, wide), BF16) for n in (self.cut, rows - self.cut)
                ]
                sums = call(
                    functools.partial(sum_kernel, self.cut),
                    (halves[0], halves[0], halves[1], halves[1]),
                    (kept, arrived),
                    scalars=0,
                )
                split = (2, -1)
                self.held = [
                    [s.reshape(split + s.shape[1:]) for s in sums[:2]],
                    [s.reshape(split + s.shape[1:]) for s in sums[2:]],
                ]
                self.held, value = wait_for(self.held, value)
                return value
            first = self.pieces((kept, arrived), slice(0, self.cut))
            second = self.pieces((kept, arrived), slice(self.cut, None))
        elif self.stage <= self.bits:
            first, second = self.held
            arrived, value = wait_for(
                (
                    swap(first[1], "dp", 1 << (self.bits + 1 - self.stage)),
                    swap(second[1], "dp", 1 << self.stage),
                ),
                value,
            )
            first, second = [first[0], arrived[0]], [second[0], arrived[1]]
        else:
            arrived, value = wait_for(
                [swap(part, "seq", j + 1) for j, part in enumerate(self.held[1:])], value
            )
            self.held = add_up([self.held[0]] + arrived)
            return value
        self.stage += 1
        if self.stage <= self.bits:
            last = self.bits - self.stage
            self.held = [
                [add_up([p[i] for p in first]).astype(BF16) for i in range(2)],
                [
                    add_up([lax.index_in_dim(p, i, last, False) for p in second]).astype(BF16)
                    for i in range(2)
                ],
            ]
        else:
            self.held = [
                jnp.concatenate(
                    [add_up([p[j] for p in half]).astype(BF16) for half in (first, second)]
                )
                for j in range(lax.axis_size("seq"))
            ]
        self.held, value = wait_for(self.held, value)
        return value


def to_lines(x):
    return jnp.pad(x, (0, -x.shape[0] % WIDE)).reshape(-1, WIDE)


def to_block(x):
    return jnp.pad(x, ((0, 0), (0, -x.shape[1] % WIDE)))


def regroup(late_all, order, rows, hidden):
    count = late_all.shape[0]
    relative = jnp.take(late_all, order, axis=0)

    def out_rows(first):
        return late_all[:, first : first + rows].reshape(BLOCKS, HIDDEN // 2, WIDE)

    def units(first):
        return relative[:, first : first + hidden].reshape(BLOCKS, HIDDEN, WIDE)

    parts = [out_rows(0), out_rows(rows)]
    parts += [units(2 * rows + i * hidden) for i in range(2 * GROUPS)]
    return jnp.concatenate(parts, 1), jnp.arange(BLOCKS, dtype=jnp.int32)


def split_late(packs, rows, hidden):
    cuts = [0, HIDDEN // 2] + [HIDDEN * i for i in range(1, 2 * GROUPS + 2)]
    sizes = [rows, rows] + [hidden] * (2 * GROUPS)
    parts = [
        packs[:, cuts[i] : cuts[i + 1]].reshape(-1, sizes[i], WIDE) for i in range(len(sizes))
    ]
    whole = jnp.concatenate(parts, 1)
    return jnp.pad(whole, ((0, 0), (0, -whole.shape[1] % 16), (0, 0)))


def split_early(packs, small, rows):
    parts = [packs[:, 24 * i : 24 * (i + 1)].reshape(-1, rows, WIDE) for i in range(5)]
    return jnp.concatenate(parts + [small.astype(BF16)], 1)


def local(
    layer_in,
    cotangent,
    valid_len,
    sep_pos,
    w_query,
    w_key,
    w_value,
    w_depth,
    w_point,
    w_kernel,
    w_convout,
    w_output,
    gain_attn,
    shift_attn,
    w_up,
    w_down,
    gain_out,
    shift_out,
):
    seq, dp = lax.axis_size("seq"), lax.axis_size("dp")
    count = seq * dp
    z, d = lax.axis_index("seq"), lax.axis_index("dp")
    core = d & 1
    me = z * dp + d
    codes = np.array(relative_codes(), np.int32)
    order = jnp.asarray(codes) ^ me
    to_absolute = (jnp.arange(count)[:, None] == order[None, :]).astype(BF16)
    rows = w_query.shape[0]
    hidden = w_up.shape[2]
    half = count // 2
    parity = jnp.stack([z & 1])
    lines = [
        to_lines(w_kernel),
        to_lines(w_depth.reshape(-1)),
        to_lines(jnp.concatenate([gain_attn, shift_attn, gain_out, shift_out])),
    ]
    starts = np.cumsum([0] + [line.shape[0] for line in lines])
    small = pad_rows(jnp.concatenate(lines), 8)
    early, tokens_a, tokens_b = call(
        prepare_kernel,
        (
            shape((5 * rows + 8, WIDE), BF16),
            shape((HALF // 2, WIDTH), BF16),
            shape((HALF // 2, WIDTH), BF16),
        ),
        (parity, layer_in, w_query, w_key, w_value, w_point, w_convout, small),
    )
    early, w_output, w_up, w_down = lax.optimization_barrier((early, w_output, w_up, w_down))
    late = pad_rows(
        jnp.concatenate(
            [
                w_output[:, :WIDE],
                w_output[:, WIDE:],
                jnp.swapaxes(w_up, 1, 2).reshape(GROUPS * hidden, WIDE),
                w_down.reshape(GROUPS * hidden, WIDE),
            ]
        ),
        16,
    )
    late_all = lax.all_gather(late, ("seq", "dp"), axis=0, tiled=False)
    parts, tokens_a, tokens_b = gather_weights(early, rows, tokens_a, tokens_b)
    token_pieces = (tokens_a, tokens_b, swap(tokens_a, "dp", 1), swap(tokens_b, "dp", 1))
    pair_info = jnp.stack([valid_len[:, 0], sep_pos[:, 0]]).astype(F32)
    place = jnp.stack([z, core, me, jnp.int32(rows)])
    offsets = np.arange(WIDTH, dtype=np.int32)
    code_rows = np.zeros((8, WIDTH), np.int32)
    code_rows[0], code_rows[1] = codes[offsets // rows], offsets % rows
    info, turned, tokens_own, matrix = call(
        permute_kernel,
        (
            shape((4,), jnp.int32),
            shape((LEN, WIDTH), BF16),
            shape((HALF, WIDTH), BF16),
            shape((WIDTH, WIDTH), BF16),
        ),
        (place, pair_info, swap(pair_info, "dp", 1)) + token_pieces + (jnp.asarray(code_rows),),
        scalars=3,
    )
    parts, cotangent = wait_for(parts, cotangent[:, 0])
    cot_a, cot_b = to_pieces(cotangent)
    parts = parts + [swap(part, "dp", 1) for part in parts]
    own, other, small_rel, q, k, v, att, stats = call(
        attend_kernel,
        (
            shape((5 * WIDE, WIDE), BF16),
            shape((5 * WIDE, WIDE), BF16),
            shape((count * 8, WIDE), BF16),
            shape((HALF, WIDE), BF16),
            shape((LEN, WIDE), BF16),
            shape((LEN, WIDE), BF16),
            shape((HALF, WIDE), BF16),
            shape((HALF, CHUNK), F32),
        ),
        (info, turned, *parts),
    )
    small_rel = small_rel.reshape(count, -1, WIDE)
    kernel_rel = small_rel[:, starts[0] : starts[1]].reshape(count, -1)[:, : w_kernel.shape[0]]
    depth_rel = small_rel[:, starts[1] : starts[2]].reshape(count, -1)[:, : w_depth.size]
    gains_rel = small_rel[:, starts[2] : starts[3]].reshape(count, -1)[:, : 4 * rows]
    kernel_abs = jnp.dot(to_absolute, kernel_rel, preferred_element_type=F32).astype(BF16)
    taps_weight = jnp.pad(
        kernel_abs.reshape(WIDE, HEADS * KERNEL), ((0, 0), (0, CHUNK - HEADS * KERNEL))
    )
    depth_weight = jnp.pad(
        depth_rel.astype(F32).reshape(count, KERNEL, rows).transpose(1, 0, 2).reshape(KERNEL, WIDTH),
        ((0, 16 - KERNEL), (0, 0)),
    )
    gains = jnp.pad(
        jnp.dot(to_absolute, gains_rel, preferred_element_type=F32)
        .reshape(count, 4, rows)
        .transpose(1, 0, 2)
        .reshape(4, WIDTH),
        ((0, 4), (0, 0)),
    )
    context, key_conv, conv_attn, depth_low, values = call(
        conv_kernel,
        (
            shape((HALF, WIDTH), BF16),
            shape((HALF, WIDE), F32),
            shape((HALF, WIDE), BF16),
            shape((HALF, WIDTH), BF16),
            shape((WIDE // CHUNK, WINDOW, CHUNK), F32),
        ),
        (info, turned, own, other, q, att, taps_weight, depth_weight),
        scratch=(
            pltpu.VMEM((WIDTH // CHUNK, WINDOW, CHUNK), F32),
            pltpu.VMEM((KERNEL, HALF, WIDE), F32),
            pltpu.VMEM((KERNEL, HALF, CHUNK), F32),
        ),
    )
    if count == BLOCKS:
        late_blocks, late_order = late_all, order
    else:
        late_blocks, late_order = regroup(late_all, order, rows, hidden)
    halves = (GROUPS, 2, BLOCKS // 2 * HIDDEN, WIDE)
    layer_a, layer_b, first_grad, context_grad, kept, sent, gain_grads = call(
        feed_kernel,
        (
            shape((HALF // 2, WIDTH), BF16),
            shape((HALF // 2, WIDTH), BF16),
            shape((HALF, WIDTH), F32),
            shape((HALF, WIDTH), BF16),
            shape((BLOCKS // 2, PACK, WIDE), BF16),
            shape((BLOCKS // 2, PACK, WIDE), BF16),
            shape((8, WIDTH), F32),
        ),
        (info, late_order, context, tokens_own, late_blocks, cot_a, cot_b, gains, matrix),
        scalars=2,
        scratch=(
            pltpu.VMEM((WIDTH, WIDTH), BF16),
            pltpu.VMEM(halves, BF16),
            pltpu.VMEM(halves, BF16),
            pltpu.VMEM((GROUPS, 2, HALF, WIDTH), BF16),
            pltpu.VMEM((GROUPS, 2, HALF, WIDTH), F32),
            pltpu.VMEM((HALF, WIDTH), F32),
            pltpu.VMEM((HALF, WIDTH), F32),
            pltpu.VMEM((HALF, WIDTH), BF16),
            pltpu.VMEM((HALF, WIDTH), BF16),
            pltpu.VMEM((HALF, WIDTH), BF16),
            pltpu.VMEM((HALF, WIDTH), F32),
            pltpu.VMEM((HALF, 1), F32),
        ),
    )
    if count != BLOCKS:
        kept, sent = split_late(kept, rows, hidden), split_late(sent, rows, hidden)
    first = Scatter(kept, sent, kept.shape[1] // 32 * 16)
    query_conv, key_low, kernel_grad, values_grad, rim_values = call(
        taps_back_kernel,
        (
            shape((HALF, WIDE), F32),
            shape((HALF, WIDE), BF16),
            shape((WIDE, CHUNK), F32),
            shape((WIDE // CHUNK, WINDOW, CHUNK), F32),
            shape((EDGE, WIDE), BF16),
        ),
        (info, q, context_grad, key_conv, conv_attn, values, taps_weight),
        scratch=(
            pltpu.VMEM((KERNEL, HALF, WIDE), F32),
            pltpu.VMEM((KERNEL, HALF, CHUNK), F32),
            pltpu.VMEM((KERNEL, HALF, CHUNK), F32),
            pltpu.VMEM((KERNEL, WINDOW, CHUNK), F32),
            pltpu.VMEM((KERNEL, HALF, CHUNK), BF16),
        ),
        micros=12,
    )
    key_low = first.step(key_low)
    layer_a, layer_b, key_low = lax.optimization_barrier((layer_a, layer_b, key_low))
    layer_a, layer_b = send_pieces(layer_a, layer_b, True)
    context_grad, key_low = lax.optimization_barrier((context_grad, key_low))
    rim_values = swap(rim_values, "dp", 1)
    query_attn, own_part, message = call(
        attend_back_kernel,
        (shape((HALF, WIDE), F32), shape((HALF, WIDTH), F32), shape((HALF, WIDTH), BF16)),
        (info, q, k, v, context, context_grad, stats),
        scratch=(pltpu.VMEM((LEN, WIDE), F32), pltpu.VMEM((LEN, WIDE), F32)),
        micros=13,
    )
    own_part = first.step(own_part)
    layer_a, own_part = wait_for(layer_a, own_part)
    own_part, key_low = wait_for(own_part, key_low)
    arrived = swap(message, "dp", 1)
    point_grad, depth_grad, back, rim_inputs = call(
        depth_back_kernel,
        (
            shape((WIDTH, WIDE), BF16),
            shape((16, WIDTH), F32),
            shape((WIDTH // CHUNK, WINDOW, CHUNK), F32),
            shape((EDGE, WIDTH), BF16),
        ),
        (info, turned, own, other, key_low, depth_low, depth_weight),
        scratch=(
            pltpu.VMEM((WIDTH // CHUNK, WINDOW, CHUNK), F32),
        ),
        micros=5,
    )
    point_grad = first.step(point_grad)
    (layer_b, rim_values), point_grad = wait_for((layer_b, rim_values), point_grad)
    rim_inputs = swap(rim_inputs, "dp", 1)

    kernel_lines = kernel_grad[:, : HEADS * KERNEL].reshape(count, -1)
    gain_lines = gain_grads[:4].reshape(4, count, rows).transpose(1, 0, 2).reshape(count, -1)
    turned_lines = lax.dot_general(
        to_absolute,
        jnp.concatenate([to_block(kernel_lines), to_block(gain_lines)], 1).astype(BF16),
        (((0,), (0,)), ((), ())),
        preferred_element_type=F32,
    )
    cut = starts[1] * WIDE
    depth_lines = to_block(
        depth_grad[:KERNEL].reshape(KERNEL, count, rows).transpose(1, 0, 2).reshape(count, -1)
    )
    small = jnp.concatenate([turned_lines[:, :cut], depth_lines, turned_lines[:, cut:]], 1)
    small = jnp.pad(small, ((0, 0), (0, 8 * WIDE - small.shape[1]))).reshape(count, 8, WIDE)
    kept, sent, low = call(
        grads_kernel,
        (
            shape((BLOCKS // 2, 128, WIDE), BF16),
            shape((BLOCKS // 2, 128, WIDE), BF16),
            shape((4, HALF, WIDE), BF16),
        ),
        (
            info,
            turned,
            query_attn,
            query_conv,
            own_part,
            arrived,
            rim_values,
            values_grad,
            point_grad,
            small[:BLOCKS],
        ),
        scratch=(pltpu.VMEM((HALF, WIDE), F32),),
        micros=8,
    )
    if count != BLOCKS:
        kept, sent = split_early(kept, small[:half], rows), split_early(sent, small[half:], rows)
    second = Scatter(kept, sent, kept.shape[1] // 32 * 16)
    rim_inputs, low = wait_for(rim_inputs, low)
    while first.stage <= first.bits:
        low = first.step(low)
    low = second.step(low)
    x_low = call(
        inputs_kernel,
        (shape((HALF // 2, WIDTH), BF16), shape((HALF // 2, WIDTH), BF16)),
        (info, own, other, matrix, depth_weight, low, rim_inputs, back, first_grad),
        scratch=(pltpu.VMEM((HALF, WIDTH), F32),),
        micros=8,
    )
    x_low = first.step(x_low)
    x_low = second.step(x_low)
    x_a, x_b = send_pieces(*x_low, True)
    x_a = second.step(x_a)
    (layer_a, layer_b), x_a = wait_for((layer_a, layer_b), x_a)
    while second.stage <= second.bits:
        second.step(())
    second.step(())
    first, second = first.held, second.held
    piece = layer_in.shape[:1] + (1,) + layer_in.shape[2:]
    layer_out = call(place_kernel, shape(piece, BF16), (parity, layer_a, layer_b))
    x_grad = call(place_kernel, shape(piece, F32), (parity, x_a, x_b))

    def part(index):
        return second[index * rows : (index + 1) * rows]

    lines = second[5 * rows : 5 * rows + 8].reshape(-1)
    kernel_at, depth_at, gain_at = (start * WIDE for start in starts[:3])
    depth_line = lines[depth_at : depth_at + w_depth.size].reshape(KERNEL, rows)
    gain_line = lines[gain_at : gain_at + 4 * rows].reshape(4, rows)
    return (
        layer_out,
        x_grad,
        part(0),
        part(1),
        part(2),
        depth_line,
        part(3),
        lines[kernel_at : kernel_at + w_kernel.shape[0]],
        part(4),
        jnp.concatenate([first[:rows], first[rows : 2 * rows]], 1),
        gain_line[0],
        gain_line[1],
        jnp.swapaxes(
            first[2 * rows : 2 * rows + GROUPS * hidden].reshape(GROUPS, hidden, WIDE), 1, 2
        ),
        first[2 * rows + GROUPS * hidden : 2 * rows + 2 * GROUPS * hidden].reshape(
            GROUPS, hidden, WIDE
        ),
        gain_line[2],
        gain_line[3],
    )


def solution(mesh):
    in_specs = (
        P(None, "dp", "seq", None),
        P(None, "dp", "seq", None),
        P(None, "dp"),
        P(None, "dp"),
        P(("seq", "dp"), None),
        P(("seq", "dp"), None),
        P(("seq", "dp"), None),
        P(None, ("seq", "dp")),
        P(("seq", "dp"), None),
        P(("seq", "dp")),
        P(("seq", "dp"), None),
        P(("seq", "dp"), None),
        P(("seq", "dp")),
        P(("seq", "dp")),
        P(None, None, ("seq", "dp")),
        P(None, ("seq", "dp"), None),
        P(("seq", "dp")),
        P(("seq", "dp")),
    )
    out_specs = (
        P(None, "dp", "seq", None),
        P(None, "dp", "seq", None),
        P(("seq", "dp"), None),
        P(("seq", "dp"), None),
        P(("seq", "dp"), None),
        P(None, ("seq", "dp")),
        P(("seq", "dp"), None),
        P(("seq", "dp")),
        P(("seq", "dp"), None),
        P(("seq", "dp"), None),
        P(("seq", "dp")),
        P(("seq", "dp")),
        P(None, None, ("seq", "dp")),
        P(None, ("seq", "dp"), None),
        P(("seq", "dp")),
        P(("seq", "dp")),
    )
    return jax.shard_map(local, mesh=mesh, in_specs=in_specs, out_specs=out_specs, check_vma=False)
```

profile of v0, /device:TPU:0, one launch (start us, length us, event | category | flops | bytes accessed | tf_op | source)
XLA Modules:
  0.0 252.2 jit_solution(17734123178252648123)
XLA Ops:
  10.1 2.2 shard_map.315
  13.1 1.6 pad_maximum_fusion.1
  14.8 5.1 %collective-permute-start.7 = (bf16[128,384]{1,0:T(8,128)(2,1)}, bf16[128,384]{1,0:T(8,128)(2,1)S(1)}, u32[]{:S(2)}, u32[]{:S(2)}) collective-permute-start(bf16[128,384]{1,0:T(8,128)(2,1)} %get-tuple-element.155), channel_id=1, source_target_pairs={{0,24},{8,16},{16,8},{24,0},{1,25},{9,17},{17,9},{25,1},{2,26},{10... | collective-permute-start | bytes 294920 | tf_op jit(solution)/shard_map/ppermute | solution.py:741
  20.5 4.5 %collective-permute-start.1 = (bf16[256,768]{1,0:T(8,128)(2,1)}, bf16[256,768]{1,0:T(8,128)(2,1)}, u32[]{:S(2)}, u32[]{:S(2)}) collective-permute-start(bf16[256,768]{1,0:T(8,128)(2,1)} %get-tuple-element.150), channel_id=1, source_target_pairs={{0,0},{1,8},{2,2},{3,10},{4,4},{5,12},{6,6},{7,14},{8,16},{9,24},{... | collective-permute-start | bytes 1179656 | tf_op jit(solution)/shard_map/ppermute | solution.py:794
  26.0 3.4 %collective-permute-done.6 = bf16[128,384]{1,0:T(8,128)(2,1)S(1)} collective-permute-done((bf16[128,384]{1,0:T(8,128)(2,1)}, bf16[128,384]{1,0:T(8,128)(2,1)S(1)}, u32[]{:S(2)}, u32[]{:S(2)}) %collective-permute-start.6) | collective-permute-done | bytes 98336 | tf_op jit(solution)/shard_map/ppermute | solution.py:741
  30.2 2.5 collective-permute-start.10
  33.8 15.3 %collective-permute-start.3 = (bf16[256,768]{1,0:T(8,128)(2,1)}, bf16[256,768]{1,0:T(8,128)(2,1)}, u32[]{:S(2)}, u32[]{:S(2)}) collective-permute-start(bf16[256,768]{1,0:T(8,128)(2,1)} %collective-permute-done.1.own_a), channel_id=1, source_target_pairs={{0,1},{1,0},{2,3},{3,2},{4,5},{5,4},{6,7},{7,6},{8,9},{9,8},{10,11... | collective-permute-start | bytes 1179656 | tf_op jit(solution)/shard_map/ppermute | solution.py:741
  51.8 1.0 dynamic-slice_bitcast_fusion
  52.7 1.9 collective-permute-start.16
  54.7 4.6 %shard_map.316 = (s32[4]{0:T(128)}, bf16[1024,768]{1,0:T(8,128)(2,1)}, bf16[512,768]{1,0:T(8,128)(2,1)}, bf16[768,768]{1,0:T(8,128)(2,1)}) custom-call(s32[4]{0:T(128)} %pad_add_fusion.place, f32[2,2]{1,0:T(2,128)} %copy-done.26, f32[2,2]{1,0:T(2,128)} %copy-done.27, bf16[256,768]{1,0:T(8,128)(2,1)} %collective-permute-done.1.own_a, ...), custom_call_target="tpu_custom_call" | custom-call | tf_op jit(solution)/shard_map/pallas_call | solution.py:49
  59.3 1.8 collective-permute-start.15
  62.1 13.0 %shard_map.317 = (bf16[1920,384]{1,0:T(8,128)(2,1)}, bf16[1920,384]{1,0:T(8,128)(2,1)}, bf16[256,384]{1,0:T(8,128)(2,1)}, bf16[512,384]{1,0:T(8,128)(2,1)}, bf16...) custom-call(s32[4]{0:T(128)} %get-tuple-element.152.info, ...), custom_call_target="tpu_custom_call" | custom-call | tf_op jit(solution)/shard_map/pallas_call | solution.py:49
  75.1 1.0 slice.361
  76.2 1.3 fusion.60
  80.3 11.6 %shard_map.318 = (bf16[512,768]{1,0:T(8,128)(2,1)}, f32[512,384]{1,0:T(8,128)}, bf16[512,384]{1,0:T(8,128)(2,1)}, bf16[512,768]{1,0:T(8,128)(2,1)}, f32[3,544,128]{2,1,0:T(8,128)}) custom-call(s32[4]{0:T(128)} %get-tuple-element.152.info, bf16[1024,768]{1,0:T(8,128)(2,1)} %get-tuple-element.153.tokens, bf16[1920,384]{1,0:T(8,128)(2,1)} %get-tuple-element.160.own, ...), custom_call_target="tpu_custom_call" | custom-call | tf_op jit(solution)/shard_map/pallas_call | solution.py:49
  91.9 7.1 %all-gather.3.cloned.1.call-done = bf16[7680,384]{1,0:T(8,128)(2,1)} async-done(((bf16[240,384]{1,0:T(8,128)(2,1)}), bf16[7680,384]{1,0:T(8,128)(2,1)}) %all-gather.3.cloned.1.call-update) | async-done | bytes 5898256 | tf_op jit(solution)/shard_map/all_gather | solution.py:978
  98.9 24.1 %shard_map.319 = (bf16[256,768]{1,0:T(8,128)(2,1)}, bf16[256,768]{1,0:T(8,128)(2,1)}, f32[512,768]{1,0:T(8,128)}, bf16[512,768]{1,0:T(8,128)(2,1)}, bf16[16,240,...) custom-call(s32[4]{0:T(128)} %get-tuple-element.152.info, s32[32]{0:T(128)} %copy-done.24, ...), custom_call_target="tpu_custom_call" | custom-call | tf_op jit(solution)/shard_map/pallas_call | solution.py:49
  123.3 13.9 %shard_map.320 = (f32[512,384]{1,0:T(8,128)}, bf16[512,384]{1,0:T(8,128)(2,1)}, f32[384,128]{1,0:T(8,128)}, f32[3,544,128]{2,1,0:T(8,128)}, bf16[16,384]{1,0:T(8,128)(2,1)}) custom-call(s32[4]{0:T(128)} %get-tuple-element.152.info, bf16[512,384]{1,0:T(8,128)(2,1)} %get-tuple-element.162.q, bf16[512,768]{1,0:T(8,128)(2,1)} %get-tuple-element.195.context_grad, ...), custom_call_target="tpu_custom_call" | custom-call | flops 1200000000 | tf_op jit(solution)/shard_map/pallas_call | solution.py:49
  137.2 1.6 copy-done
  138.9 4.6 %shard_map.321 = (bf16[8,112,384]{2,1,0:T(8,128)(2,1)}, bf16[8,112,384]{2,1,0:T(8,128)(2,1)}, bf16[8,128,384]{2,1,0:T(8,128)(2,1)}, bf16[8,128,384]{2,1,0:T(8,128)(2,1)}) custom-call(bf16[16,240,384]{2,1,0:T(8,128)(2,1)} %get-tuple-element.174.kept, bf16[16,240,384]{2,1,0:T(8,128)(2,1)} %copy-done), custom_call_target="tpu_custom_call" | custom-call | tf_op jit(solution)/shard_map/pallas_call | solution.py:49
  143.5 1.4 collective-permute-start.20
  146.6 1.8 collective-permute-start.18
  148.5 12.5 %shard_map.322 = (f32[512,384]{1,0:T(8,128)}, f32[512,768]{1,0:T(8,128)}, bf16[512,768]{1,0:T(8,128)(2,1)}) custom-call(s32[4]{0:T(128)} %get-tuple-element.152.info, bf16[512,384]{1,0:T(8,128)(2,1)} %get-tuple-element.162.q, bf16[1024,384]{1,0:T(8,128)(2,1)} %get-tuple-element.192.k, bf16[1024,384]{1,0:T(8,128)(2,1)} %get-tuple-element.193.v, ...), custom_call_target="tpu_custom_call" | custom-call | flops 1300000000 | tf_op jit(solution)/shard_map/pallas_call | solution.py:49
  161.0 1.4 collective-permute-done.19
  162.4 1.0 collective-permute-done.20
  164.5 1.4 collective-permute-start.23
  167.5 1.8 collective-permute-start.21
  169.8 6.3 %shard_map.323 = (bf16[768,384]{1,0:T(8,128)(2,1)}, f32[16,768]{1,0:T(8,128)}, f32[6,544,128]{2,1,0:T(8,128)}, bf16[16,768]{1,0:T(8,128)(2,1)}) custom-call(s32[4]{0:T(128)} %get-tuple-element.152.info, bf16[1024,768]{1,0:T(8,128)(2,1)} %get-tuple-element.153.tokens, bf16[1920,384]{1,0:T(8,128)(2,1)} %get-tuple-element.160.own, ...), custom_call_target="tpu_custom_call" | custom-call | flops 500000000 | tf_op jit(solution)/shard_map/pallas_call | solution.py:49
  178.1 1.1 fusion.19
  179.4 1.3 collective-permute-done.21.second
  181.6 7.2 %shard_map.324 = (bf16[16,128,384]{2,1,0:T(8,128)(2,1)}, bf16[16,128,384]{2,1,0:T(8,128)(2,1)}, bf16[4,512,384]{2,1,0:T(8,128)(2,1)}) custom-call(s32[4]{0:T(128)} %get-tuple-element.152.info, bf16[1024,768]{1,0:T(8,128)(2,1)} %get-tuple-element.153.tokens, f32[512,384]{1,0:T(8,128)} %get-tuple-element.220.query_attn, ...), custom_call_target="tpu_custom_call" | custom-call | flops 800000000 | tf_op jit(solution)/shard_map/pallas_call | solution.py:49
  189.2 2.1 collective-permute-start.31
  191.4 1.8 collective-permute-start.32
  193.2 1.2 collective-permute-done.27.rim_inputs
  194.4 1.1 copy-done.1
  195.5 3.2 %shard_map.325 = (bf16[8,64,384]{2,1,0:T(8,128)(2,1)}, bf16[8,64,384]{2,1,0:T(8,128)(2,1)}, bf16[8,64,384]{2,1,0:T(8,128)(2,1)}, bf16[8,64,384]{2,1,0:T(8,128)(2,1)}) custom-call(bf16[16,128,384]{2,1,0:T(8,128)(2,1)} %get-tuple-element.230.kept, bf16[16,128,384]{2,1,0:T(8,128)(2,1)} %copy-done.1), custom_call_target="tpu_custom_call" | custom-call | tf_op jit(solution)/shard_map/pallas_call | solution.py:49
  198.7 1.6 collective-permute-start.28
  200.8 9.3 %shard_map.326 = (bf16[256,768]{1,0:T(8,128)(2,1)}, bf16[256,768]{1,0:T(8,128)(2,1)}) custom-call(s32[4]{0:T(128)} %get-tuple-element.152.info, bf16[1920,384]{1,0:T(8,128)(2,1)} %get-tuple-element.160.own, bf16[1920,384]{1,0:T(8,128)(2,1)} %get-tuple-element.161.other, bf16[768,768]{1,0:T(8,128)(2,1)} %get-tuple-element.171.matrix, ...), custom_call_target="tpu_custom_call" | custom-call | flops 800000000 | tf_op jit(solution)/shard_map/pallas_call | solution.py:49
  210.3 1.2 collective-permute-done.29
  213.1 1.1 collective-permute-start.33
  215.0 2.1 collective-permute-start.36
  217.1 3.5 %collective-permute-done.33 = bf16[4,64,384]{2,1,0:T(8,128)(2,1)S(1)} collective-permute-done((bf16[4,64,384]{2,1,0:T(8,128)(2,1)S(1)}, bf16[4,64,384]{2,1,0:T(8,128)(2,1)S(1)}, u32[]{:S(2)}, u32[]{:S(2)}) %collective-permute-start.33) | collective-permute-done | bytes 196640 | tf_op jit(solution)/shard_map/ppermute | solution.py:741
  220.6 1.3 collective-permute-done.34
  222.1 5.1 %collective-permute-start.37 = (bf16[128,384]{1,0:T(8,128)(2,1)S(1)}, bf16[128,384]{1,0:T(8,128)(2,1)S(1)}, u32[]{:S(2)}, u32[]{:S(2)}) collective-permute-start(bf16[128,384]{1,0:T(8,128)(2,1)S(1)} %pad_maximum_fusion.7), channel_id=1, source_target_pairs={{0,8},{8,0},{16,24},{24,16},{1,9},{9,1},{17,25},{25,17},{2,10},{10... | collective-permute-start | bytes 294920 | tf_op jit(solution)/shard_map/ppermute | solution.py:741
  227.2 2.4 collective-permute-start.39
  230.3 2.0 shard_map.327
  232.3 7.0 %collective-permute-done.36.second = bf16[256,768]{1,0:T(8,128)(2,1)S(1)} collective-permute-done((bf16[256,768]{1,0:T(8,128)(2,1)S(1)}, bf16[256,768]{1,0:T(8,128)(2,1)S(1)}, u32[]{:S(2)}, u32[]{:S(2)}) %collective-permute-start.36) | collective-permute-done | bytes 393248 | tf_op jit(solution)/shard_map/ppermute | solution.py:794
  240.1 2.4 shard_map.328
  (205 shorter events, 29.5 us)
Async XLA Ops:
  7.2 91.7 %all-gather.3.cloned.1.call-start = ((), (), s32[]{:S(2)}) async-start(), calls=%async_computation | async-start | bytes 6082560 | tf_op jit(solution)/shard_map/all_gather | solution.py:978
  12.3 36.8 %copy-start.28 = (s32[2,1]{0,1:T(1,128)S(1)}, s32[2,1]{0,1:T(1,128)}, u32[]{:S(2)}) copy-start(s32[2,1]{0,1:T(1,128)} %param.23) | copy-start | bytes 28
  12.3 36.8 %copy-start.29 = (s32[2,1]{0,1:T(1,128)S(1)}, s32[2,1]{0,1:T(1,128)}, u32[]{:S(2)}) copy-start(s32[2,1]{0,1:T(1,128)} %param.22) | copy-start | bytes 28
  12.3 39.5 %copy-start.35 = (s32[32]{0:T(128)S(1)}, s32[32]{0:T(128)}, u32[]{:S(2)}) copy-start(s32[32]{0:T(128)} %constant.34.clone) | copy-start | bytes 388
  12.3 39.5 %copy-start.3 = (bf16[2,1,256,768]{3,2,1,0:T(8,128)(2,1)S(1)}, bf16[2,1,256,768]{3,2,1,0:T(8,128)(2,1)}, u32[]{:S(2)}) copy-start(bf16[2,1,256,768]{3,2,1,0:T(8,128)(2,1)} %param.21) | copy-start | bytes 2359300
  14.8 11.1 %collective-permute-start.7 = (bf16[128,384]{1,0:T(8,128)(2,1)}, bf16[128,384]{1,0:T(8,128)(2,1)S(1)}, u32[]{:S(2)}, u32[]{:S(2)}) collective-permute-start(bf16[128,384]{1,0:T(8,128)(2,1)} %get-tuple-element.155), channel_id=1, source_target_pairs={{0,24},{8,16},{16,8},{24,0},{1,25},{9,17},{17,9},{25,1},{2,26},{10... | collective-permute-start | bytes 294920 | tf_op jit(solution)/shard_map/ppermute | solution.py:741
  19.9 9.4 %collective-permute-start.6 = (bf16[128,384]{1,0:T(8,128)(2,1)}, bf16[128,384]{1,0:T(8,128)(2,1)S(1)}, u32[]{:S(2)}, u32[]{:S(2)}) collective-permute-start(bf16[128,384]{1,0:T(8,128)(2,1)} %get-tuple-element.155), channel_id=1, source_target_pairs={{0,16},{8,24},{16,0},{24,8},{1,17},{9,25},{17,1},{25,9},{2,18},{10... | collective-permute-start | bytes 294920 | tf_op jit(solution)/shard_map/ppermute | solution.py:741
  19.9 9.4 %collective-permute-start.5 = (bf16[128,384]{1,0:T(8,128)(2,1)}, bf16[128,384]{1,0:T(8,128)(2,1)S(1)}, u32[]{:S(2)}, u32[]{:S(2)}) collective-permute-start(bf16[128,384]{1,0:T(8,128)(2,1)} %get-tuple-element.155), channel_id=1, source_target_pairs={{0,8},{8,0},{16,24},{24,16},{1,9},{9,1},{17,25},{25,17},{2,10},{10... | collective-permute-start | bytes 294920 | tf_op jit(solution)/shard_map/ppermute | solution.py:741
  20.5 13.2 %collective-permute-start.1 = (bf16[256,768]{1,0:T(8,128)(2,1)}, bf16[256,768]{1,0:T(8,128)(2,1)}, u32[]{:S(2)}, u32[]{:S(2)}) collective-permute-start(bf16[256,768]{1,0:T(8,128)(2,1)} %get-tuple-element.150), channel_id=1, source_target_pairs={{0,0},{1,8},{2,2},{3,10},{4,4},{5,12},{6,6},{7,14},{8,16},{9,24},{... | collective-permute-start | bytes 1179656 | tf_op jit(solution)/shard_map/ppermute | solution.py:794
  25.0 24.1 %collective-permute-start.2 = (bf16[256,768]{1,0:T(8,128)(2,1)}, bf16[256,768]{1,0:T(8,128)(2,1)}, u32[]{:S(2)}, u32[]{:S(2)}) collective-permute-start(bf16[256,768]{1,0:T(8,128)(2,1)} %get-tuple-element.151), channel_id=1, source_target_pairs={{0,16},{1,24},{2,18},{3,26},{4,20},{5,28},{6,22},{7,30},{8,0},{9,8... | collective-permute-start | bytes 1179656 | tf_op jit(solution)/shard_map/ppermute | solution.py:794
  30.2 29.1 %copy-start.2 = (bf16[512,384]{1,0:T(8,128)(2,1)}, bf16[512,384]{1,0:T(8,128)(2,1)S(1)}, u32[]{:S(2)}) copy-start(bf16[512,384]{1,0:T(8,128)(2,1)S(1)} %constant_dynamic-update-slice_fusion.refs_0_) | copy-start | bytes 1179652
  30.2 19.0 %collective-permute-start.10 = (bf16[512,384]{1,0:T(8,128)(2,1)S(1)}, bf16[512,384]{1,0:T(8,128)(2,1)S(1)}, u32[]{:S(2)}, u32[]{:S(2)}) collective-permute-start(bf16[512,384]{1,0:T(8,128)(2,1)S(1)} %constant_dynamic-update-slice_fusion.refs_0_), channel_id=1, source_target_pairs={{0,6},{1,7},{2,4},{3,5},{4,2},{5,3},{6,0},{7,1},{8,14},{9,15},{10,... | collective-permute-start | bytes 1179656 | tf_op jit(solution)/shard_map/ppermute | solution.py:741
  32.7 17.0 %collective-permute-start.9 = (bf16[512,384]{1,0:T(8,128)(2,1)S(1)}, bf16[512,384]{1,0:T(8,128)(2,1)S(1)}, u32[]{:S(2)}, u32[]{:S(2)}) collective-permute-start(bf16[512,384]{1,0:T(8,128)(2,1)S(1)} %constant_dynamic-update-slice_fusion.refs_0_), channel_id=1, source_target_pairs={{0,4},{1,5},{2,6},{3,7},{4,0},{5,1},{6,2},{7,3},{8,12},{9,13},{10,... | collective-permute-start | bytes 1179656 | tf_op jit(solution)/shard_map/ppermute | solution.py:741
  33.2 16.5 %collective-permute-start.8 = (bf16[512,384]{1,0:T(8,128)(2,1)S(1)}, bf16[512,384]{1,0:T(8,128)(2,1)S(1)}, u32[]{:S(2)}, u32[]{:S(2)}) collective-permute-start(bf16[512,384]{1,0:T(8,128)(2,1)S(1)} %constant_dynamic-update-slice_fusion.refs_0_), channel_id=1, source_target_pairs={{0,2},{1,3},{2,0},{3,1},{4,6},{5,7},{6,4},{7,5},{8,10},{9,11},{10,... | collective-permute-start | bytes 1179656 | tf_op jit(solution)/shard_map/ppermute | solution.py:741
  33.8 17.1 %collective-permute-start.3 = (bf16[256,768]{1,0:T(8,128)(2,1)}, bf16[256,768]{1,0:T(8,128)(2,1)}, u32[]{:S(2)}, u32[]{:S(2)}) collective-permute-start(bf16[256,768]{1,0:T(8,128)(2,1)} %collective-permute-done.1.own_a), channel_id=1, source_target_pairs={{0,1},{1,0},{2,3},{3,2},{4,5},{5,4},{6,7},{7,6},{8,9},{9,8},{10,11... | collective-permute-start | bytes 1179656 | tf_op jit(solution)/shard_map/ppermute | solution.py:741
  49.1 1.3 collective-permute-start
  49.2 3.5 %collective-permute-start.4 = (bf16[256,768]{1,0:T(8,128)(2,1)}, bf16[256,768]{1,0:T(8,128)(2,1)}, u32[]{:S(2)}, u32[]{:S(2)}) collective-permute-start(bf16[256,768]{1,0:T(8,128)(2,1)} %collective-permute-done.2.own_b), channel_id=1, source_target_pairs={{0,1},{1,0},{2,3},{3,2},{4,5},{5,4},{6,7},{7,6},{8,9},{9,8},{10,11... | collective-permute-start | bytes 1179656 | tf_op jit(solution)/shard_map/ppermute | solution.py:741
  49.7 9.6 %collective-permute-start.11 = (bf16[512,384]{1,0:T(8,128)(2,1)S(1)}, bf16[512,384]{1,0:T(8,128)(2,1)S(1)}, u32[]{:S(2)}, u32[]{:S(2)}) collective-permute-start(bf16[512,384]{1,0:T(8,128)(2,1)S(1)} %constant_dynamic-update-slice_fusion.refs_0_), channel_id=1, source_target_pairs={{0,1},{1,0},{2,3},{3,2},{4,5},{5,4},{6,7},{7,6},{8,9},{9,8},{10,11... | collective-permute-start | bytes 1179656 | tf_op jit(solution)/shard_map/ppermute | solution.py:741
  49.9 11.2 %collective-permute-start.12 = (bf16[512,384]{1,0:T(8,128)(2,1)S(1)}, bf16[512,384]{1,0:T(8,128)(2,1)S(1)}, u32[]{:S(2)}, u32[]{:S(2)}) collective-permute-start(bf16[512,384]{1,0:T(8,128)(2,1)S(1)} %collective-permute-done.8.refs_1_), channel_id=1, source_target_pairs={{0,1},{1,0},{2,3},{3,2},{4,5},{5,4},{6,7},{7,6},{8,9},{9,8},{10,11... | collective-permute-start | bytes 1179656 | tf_op jit(solution)/shard_map/ppermute | solution.py:741
  50.5 10.7 %collective-permute-start.13 = (bf16[512,384]{1,0:T(8,128)(2,1)S(1)}, bf16[512,384]{1,0:T(8,128)(2,1)S(1)}, u32[]{:S(2)}, u32[]{:S(2)}) collective-permute-start(bf16[512,384]{1,0:T(8,128)(2,1)S(1)} %collective-permute-done.9.refs_2_), channel_id=1, source_target_pairs={{0,1},{1,0},{2,3},{3,2},{4,5},{5,4},{6,7},{7,6},{8,9},{9,8},{10,11... | collective-permute-start | bytes 1179656 | tf_op jit(solution)/shard_map/ppermute | solution.py:741
  50.8 10.4 %collective-permute-start.14 = (bf16[512,384]{1,0:T(8,128)(2,1)S(1)}, bf16[512,384]{1,0:T(8,128)(2,1)}, u32[]{:S(2)}, u32[]{:S(2)}) collective-permute-start(bf16[512,384]{1,0:T(8,128)(2,1)S(1)} %collective-permute-done.10.refs_3_), channel_id=1, source_target_pairs={{0,1},{1,0},{2,3},{3,2},{4,5},{5,4},{6,7},{7,6},{8,9},{9,8},{10,11... | collective-permute-start | bytes 1179656 | tf_op jit(solution)/shard_map/ppermute | solution.py:741
  51.8 26.9 %copy-start.24 = (s32[32]{0:T(128)}, s32[32]{0:T(128)S(1)}, u32[]{:S(2)}) copy-start(s32[32]{0:T(128)S(1)} %broadcast_xor_fusion.order) | copy-start | bytes 388
  52.7 39.1 %collective-permute-start.16 = (bf16[256,768]{1,0:T(8,128)(2,1)}, bf16[256,768]{1,0:T(8,128)(2,1)S(1)}, u32[]{:S(2)}, u32[]{:S(2)}) collective-permute-start(bf16[256,768]{1,0:T(8,128)(2,1)} %get-tuple-element.296), channel_id=1, source_target_pairs={{0,16},{1,24},{2,18},{3,26},{4,20},{5,28},{6,22},{7,30},{8,0},{9,8... | collective-permute-start | bytes 1179656 | tf_op jit(solution)/shard_map/ppermute | solution.py:794
  59.3 32.5 %collective-permute-start.15 = (bf16[256,768]{1,0:T(8,128)(2,1)}, bf16[256,768]{1,0:T(8,128)(2,1)S(1)}, u32[]{:S(2)}, u32[]{:S(2)}) collective-permute-start(bf16[256,768]{1,0:T(8,128)(2,1)} %get-tuple-element.297), channel_id=1, source_target_pairs={{0,0},{1,8},{2,2},{3,10},{4,4},{5,12},{6,6},{7,14},{8,16},{9,24},{... | collective-permute-start | bytes 1179656 | tf_op jit(solution)/shard_map/ppermute | solution.py:794
  123.0 14.2 %collective-permute-start.17 = (bf16[16,240,384]{2,1,0:T(8,128)(2,1)}, bf16[16,240,384]{2,1,0:T(8,128)(2,1)S(1)}, u32[]{:S(2)}, u32[]{:S(2)}) collective-permute-start(bf16[16,240,384]{2,1,0:T(8,128)(2,1)} %get-tuple-element.175), channel_id=1, source_target_pairs={{0,1},{1,0},{2,3},{3,2},{4,5},{5,4},{6,7},{7,6},{8,9},{9,8},{10,11... | collective-permute-start | bytes 8847368 | tf_op jit(solution)/shard_map/ppermute | solution.py:741
  143.5 19.9 %collective-permute-start.20 = (bf16[2,4,128,384]{3,2,1,0:T(8,128)(2,1)}, bf16[2,4,128,384]{3,2,1,0:T(8,128)(2,1)S(1)}, u32[]{:S(2)}, u32[]{:S(2)}) collective-permute-start(bf16[2,4,128,384]{3,2,1,0:T(8,128)(2,1)} %bitcast.127), channel_id=1, source_target_pairs={{0,2},{1,3},{2,0},{3,1},{4,6},{5,7},{6,4},{7,5},{8,10},{9,11},{10,... | collective-permute-start | bytes 2359304 | tf_op jit(solution)/shard_map/ppermute | solution.py:741
  144.9 17.5 %collective-permute-start.19 = (bf16[2,4,112,384]{3,2,1,0:T(8,128)(2,1)}, bf16[2,4,112,384]{3,2,1,0:T(8,128)(2,1)S(1)}, u32[]{:S(2)}, u32[]{:S(2)}) collective-permute-start(bf16[2,4,112,384]{3,2,1,0:T(8,128)(2,1)} %bitcast.128), channel_id=1, source_target_pairs={{0,4},{1,5},{2,6},{3,7},{4,0},{5,1},{6,2},{7,3},{8,12},{9,13},{10,... | collective-permute-start | bytes 2064392 | tf_op jit(solution)/shard_map/ppermute | solution.py:741
  146.6 22.7 %collective-permute-start.18 = (bf16[256,768]{1,0:T(8,128)(2,1)}, bf16[256,768]{1,0:T(8,128)(2,1)S(1)}, u32[]{:S(2)}, u32[]{:S(2)}) collective-permute-start(bf16[256,768]{1,0:T(8,128)(2,1)} %get-tuple-element.188), channel_id=1, source_target_pairs={{0,0},{8,1},{2,2},{10,3},{4,4},{12,5},{6,6},{14,7},{16,8},{24,9},{... | collective-permute-start | bytes 1179656 | tf_op jit(solution)/shard_map/ppermute | solution.py:794
  164.5 13.5 %collective-permute-start.23 = (bf16[4,112,384]{2,1,0:T(8,128)(2,1)}, bf16[4,112,384]{2,1,0:T(8,128)(2,1)}, u32[]{:S(2)}, u32[]{:S(2)}) collective-permute-start(bf16[4,112,384]{2,1,0:T(8,128)(2,1)} %get-tuple-element.207), channel_id=1, source_target_pairs={{0,2},{1,3},{2,0},{3,1},{4,6},{5,7},{6,4},{7,5},{8,10},{9,11},{10,... | collective-permute-start | bytes 1032200 | tf_op jit(solution)/shard_map/ppermute | solution.py:741
  166.0 12.1 %collective-permute-start.24 = (bf16[4,128,384]{2,1,0:T(8,128)(2,1)S(1)}, bf16[4,128,384]{2,1,0:T(8,128)(2,1)S(1)}, u32[]{:S(2)}, u32[]{:S(2)}) collective-permute-start(bf16[4,128,384]{2,1,0:T(8,128)(2,1)S(1)} %get-tuple-element.208), channel_id=1, source_target_pairs={{0,4},{1,5},{2,6},{3,7},{4,0},{5,1},{6,2},{7,3},{8,12},{9,13},{10,... | collective-permute-start | bytes 1179656 | tf_op jit(solution)/shard_map/ppermute | solution.py:741
  166.8 12.6 %collective-permute-start.22 = (bf16[16,384]{1,0:T(8,128)(2,1)S(1)}, bf16[16,384]{1,0:T(8,128)(2,1)S(1)}, u32[]{:S(2)}, u32[]{:S(2)}) collective-permute-start(bf16[16,384]{1,0:T(8,128)(2,1)S(1)} %copy-done.34), channel_id=1, source_target_pairs={{0,1},{1,0},{2,3},{3,2},{4,5},{5,4},{6,7},{7,6},{8,9},{9,8},{10,11... | collective-permute-start | bytes 36872 | tf_op jit(solution)/shard_map/ppermute | solution.py:741
  167.5 13.1 %collective-permute-start.21 = (bf16[256,768]{1,0:T(8,128)(2,1)S(1)}, bf16[256,768]{1,0:T(8,128)(2,1)S(1)}, u32[]{:S(2)}, u32[]{:S(2)}) collective-permute-start(bf16[256,768]{1,0:T(8,128)(2,1)S(1)} %copy-done.30), channel_id=1, source_target_pairs={{16,0},{24,1},{18,2},{26,3},{20,4},{28,5},{22,6},{30,7},{0,8},{8,9... | collective-permute-start | bytes 1179656 | tf_op jit(solution)/shard_map/ppermute | solution.py:794
  169.3 11.4 %collective-permute-start.25 = (bf16[512,768]{1,0:T(8,128)(2,1)}, bf16[512,768]{1,0:T(8,128)(2,1)S(1)}, u32[]{:S(2)}, u32[]{:S(2)}) collective-permute-start(bf16[512,768]{1,0:T(8,128)(2,1)} %get-tuple-element.223), channel_id=1, source_target_pairs={{0,1},{1,0},{2,3},{3,2},{4,5},{5,4},{6,7},{7,6},{8,9},{9,8},{10,11... | collective-permute-start | bytes 2359304 | tf_op jit(solution)/shard_map/ppermute | solution.py:741
  180.7 18.1 %copy-start.18 = (bf16[256,768]{1,0:T(8,128)(2,1)}, bf16[256,768]{1,0:T(8,128)(2,1)S(1)}, u32[]{:S(2)}) copy-start(bf16[256,768]{1,0:T(8,128)(2,1)S(1)} %collective-permute-done.21.second) | copy-start | bytes 1179652
  188.8 5.6 %collective-permute-start.26 = (bf16[16,128,384]{2,1,0:T(8,128)(2,1)}, bf16[16,128,384]{2,1,0:T(8,128)(2,1)S(1)}, u32[]{:S(2)}, u32[]{:S(2)}) collective-permute-start(bf16[16,128,384]{2,1,0:T(8,128)(2,1)} %get-tuple-element.231), channel_id=1, source_target_pairs={{0,1},{1,0},{2,3},{3,2},{4,5},{5,4},{6,7},{7,6},{8,9},{9,8},{10,11... | collective-permute-start | bytes 4718600 | tf_op jit(solution)/shard_map/ppermute | solution.py:741
  188.8 21.3 %collective-permute-start.30 = (bf16[240,384]{1,0:T(8,128)(2,1)S(1)}, bf16[240,384]{1,0:T(8,128)(2,1)S(1)}, u32[]{:S(2)}, u32[]{:S(2)}) collective-permute-start(bf16[240,384]{1,0:T(8,128)(2,1)S(1)} %pad_maximum_fusion.3), channel_id=1, source_target_pairs={{0,8},{8,0},{16,24},{24,16},{1,9},{9,1},{17,25},{25,17},{2,10},{10... | collective-permute-start | bytes 552968 | tf_op jit(solution)/shard_map/ppermute | solution.py:741
  189.2 20.9 %collective-permute-start.31 = (bf16[240,384]{1,0:T(8,128)(2,1)S(1)}, bf16[240,384]{1,0:T(8,128)(2,1)S(1)}, u32[]{:S(2)}, u32[]{:S(2)}) collective-permute-start(bf16[240,384]{1,0:T(8,128)(2,1)S(1)} %pad_maximum_fusion.4), channel_id=1, source_target_pairs={{0,16},{8,24},{16,0},{24,8},{1,17},{9,25},{17,1},{25,9},{2,18},{10... | collective-permute-start | bytes 552968 | tf_op jit(solution)/shard_map/ppermute | solution.py:741
  191.4 18.8 %collective-permute-start.32 = (bf16[240,384]{1,0:T(8,128)(2,1)S(1)}, bf16[240,384]{1,0:T(8,128)(2,1)S(1)}, u32[]{:S(2)}, u32[]{:S(2)}) collective-permute-start(bf16[240,384]{1,0:T(8,128)(2,1)S(1)} %pad_maximum_fusion.5), channel_id=1, source_target_pairs={{0,24},{8,16},{16,8},{24,0},{1,25},{9,17},{17,9},{25,1},{2,26},{10... | collective-permute-start | bytes 552968 | tf_op jit(solution)/shard_map/ppermute | solution.py:741
  193.2 1.2 collective-permute-start.27
  198.7 11.5 %collective-permute-start.28 = (bf16[2,4,64,384]{3,2,1,0:T(8,128)(2,1)}, bf16[2,4,64,384]{3,2,1,0:T(8,128)(2,1)S(1)}, u32[]{:S(2)}, u32[]{:S(2)}) collective-permute-start(bf16[2,4,64,384]{3,2,1,0:T(8,128)(2,1)} %bitcast.130), channel_id=1, source_target_pairs={{0,4},{1,5},{2,6},{3,7},{4,0},{5,1},{6,2},{7,3},{8,12},{9,13},{10,... | collective-permute-start | bytes 1179656 | tf_op jit(solution)/shard_map/ppermute | solution.py:741
  200.3 11.1 %collective-permute-start.29 = (bf16[2,4,64,384]{3,2,1,0:T(8,128)(2,1)}, bf16[2,4,64,384]{3,2,1,0:T(8,128)(2,1)S(1)}, u32[]{:S(2)}, u32[]{:S(2)}) collective-permute-start(bf16[2,4,64,384]{3,2,1,0:T(8,128)(2,1)} %bitcast.129), channel_id=1, source_target_pairs={{0,2},{1,3},{2,0},{3,1},{4,6},{5,7},{6,4},{7,5},{8,10},{9,11},{10,... | collective-permute-start | bytes 1179656 | tf_op jit(solution)/shard_map/ppermute | solution.py:741
  211.7 10.3 %collective-permute-start.35 = (bf16[256,768]{1,0:T(8,128)(2,1)S(1)}, bf16[256,768]{1,0:T(8,128)(2,1)S(1)}, u32[]{:S(2)}, u32[]{:S(2)}) collective-permute-start(bf16[256,768]{1,0:T(8,128)(2,1)S(1)} %copy-done.32), channel_id=1, source_target_pairs={{0,0},{8,1},{2,2},{10,3},{4,4},{12,5},{6,6},{14,7},{16,8},{24,9},{... | collective-permute-start | bytes 1179656 | tf_op jit(solution)/shard_map/ppermute | solution.py:794
  213.1 7.5 %collective-permute-start.33 = (bf16[4,64,384]{2,1,0:T(8,128)(2,1)S(1)}, bf16[4,64,384]{2,1,0:T(8,128)(2,1)S(1)}, u32[]{:S(2)}, u32[]{:S(2)}) collective-permute-start(bf16[4,64,384]{2,1,0:T(8,128)(2,1)S(1)} %get-tuple-element.261), channel_id=1, source_target_pairs={{0,2},{1,3},{2,0},{3,1},{4,6},{5,7},{6,4},{7,5},{8,10},{9,11},{10,... | collective-permute-start | bytes 589832 | tf_op jit(solution)/shard_map/ppermute | solution.py:741
  214.2 7.8 %collective-permute-start.34 = (bf16[4,64,384]{2,1,0:T(8,128)(2,1)S(1)}, bf16[4,64,384]{2,1,0:T(8,128)(2,1)S(1)}, u32[]{:S(2)}, u32[]{:S(2)}) collective-permute-start(bf16[4,64,384]{2,1,0:T(8,128)(2,1)S(1)} %get-tuple-element.262), channel_id=1, source_target_pairs={{0,4},{1,5},{2,6},{3,7},{4,0},{5,1},{6,2},{7,3},{8,12},{9,13},{10,... | collective-permute-start | bytes 589832 | tf_op jit(solution)/shard_map/ppermute | solution.py:741
  215.0 24.3 %collective-permute-start.36 = (bf16[256,768]{1,0:T(8,128)(2,1)S(1)}, bf16[256,768]{1,0:T(8,128)(2,1)S(1)}, u32[]{:S(2)}, u32[]{:S(2)}) collective-permute-start(bf16[256,768]{1,0:T(8,128)(2,1)S(1)} %copy-done.31), channel_id=1, source_target_pairs={{16,0},{24,1},{18,2},{26,3},{20,4},{28,5},{22,6},{30,7},{0,8},{8,9... | collective-permute-start | bytes 1179656 | tf_op jit(solution)/shard_map/ppermute | solution.py:794
  222.1 20.3 %collective-permute-start.37 = (bf16[128,384]{1,0:T(8,128)(2,1)S(1)}, bf16[128,384]{1,0:T(8,128)(2,1)S(1)}, u32[]{:S(2)}, u32[]{:S(2)}) collective-permute-start(bf16[128,384]{1,0:T(8,128)(2,1)S(1)} %pad_maximum_fusion.7), channel_id=1, source_target_pairs={{0,8},{8,0},{16,24},{24,16},{1,9},{9,1},{17,25},{25,17},{2,10},{10... | collective-permute-start | bytes 294920 | tf_op jit(solution)/shard_map/ppermute | solution.py:741
  227.2 15.2 %collective-permute-start.38 = (bf16[128,384]{1,0:T(8,128)(2,1)S(1)}, bf16[128,384]{1,0:T(8,128)(2,1)S(1)}, u32[]{:S(2)}, u32[]{:S(2)}) collective-permute-start(bf16[128,384]{1,0:T(8,128)(2,1)S(1)} %pad_maximum_fusion.8), channel_id=1, source_target_pairs={{0,16},{8,24},{16,0},{24,8},{1,17},{9,25},{17,1},{25,9},{2,18},{10... | collective-permute-start | bytes 294920 | tf_op jit(solution)/shard_map/ppermute | solution.py:741
  227.2 15.2 %collective-permute-start.39 = (bf16[128,384]{1,0:T(8,128)(2,1)S(1)}, bf16[128,384]{1,0:T(8,128)(2,1)S(1)}, u32[]{:S(2)}, u32[]{:S(2)}) collective-permute-start(bf16[128,384]{1,0:T(8,128)(2,1)S(1)} %pad_maximum_fusion.9), channel_id=1, source_target_pairs={{0,24},{8,16},{16,8},{24,0},{1,25},{9,17},{17,9},{25,1},{2,26},{10... | collective-permute-start | bytes 294920 | tf_op jit(solution)/shard_map/ppermute | solution.py:741
  (29 other events, 151.2 us)
Sparse Core Ops, SparseCore 0:
  14.9 83.9 all-gather.2
where the time goes:
time: 256 us; the launch traced here: 252 us
  Pallas kernels  117 us (46%)
  starting transfers between devices  62.6 us (24%)
  waiting for transfers between devices  28.4 us (11%)
  local copies, waits for them, and re-layouts  21 us (8%)
  between operations  15.1 us (6%)
  other arithmetic  7.84 us (3%)
    pallas_call x14, Pallas kernels, call(): pl.pallas_call(kernel, out_shape=out_shape, in_specs=[smem] * scalars + [...  117 us
    ppermute x32, starting transfers between devices, swap(): return lax.ppermute(x, axis, [(i, i ^ mask) for i in range(count)])  47.9 us
    ppermute x32, waiting for transfers between devices, swap(): return lax.ppermute(x, axis, [(i, i ^ mask) for i in range(count)])  13.1 us
    ppermute x4, starting transfers between devices, send_pieces(): lax.ppermute(a, ('seq', 'dp'), first)  8.8 us
    ppermute x4, waiting for transfers between devices, send_pieces(): lax.ppermute(b, ('seq', 'dp'), second)  8.23 us
    all_gather x1, waiting for transfers between devices, local(): late_all = lax.all_gather(late, ('seq', 'dp'), axis=0, tiled=False)  7.06 us
    unnamed x78, local copies, waits for them, and re-layouts  7.03 us
    ppermute x4, starting transfers between devices, send_pieces(): lax.ppermute(b, ('seq', 'dp'), second)  5.84 us
  transfers between devices with their start and end apart: 41, of which 11 were waited for; matrix products, arithmetic and copies ran while one was open for 6% of the time, Pallas kernels for 31%

commit v1 on v0

--- a/solution.py
+++ b/solution.py
@@ -109,6 +109,15 @@
     for i in range(3):
         pair = jnp.concatenate(pieces[2 * i : 2 * i + 2], 0)
         early[2 * i * rows : 2 * i * rows + pair.shape[0], :] = pair.astype(BF16)
+
+
+def pack_kernel(out, up, down, late):
+    half = HIDDEN // 2
+    sides = out[...].astype(F32)
+    late[0:HIDDEN, :] = jnp.concatenate([sides[:half, :WIDE], sides[:half, WIDE:]], 0).astype(BF16)
+    for g in range(GROUPS):
+        late[(1 + g) * HIDDEN : (2 + g) * HIDDEN, :] = up[g]
+        late[(3 + g) * HIDDEN : (4 + g) * HIDDEN, :] = down[g]
 
 
 def permute_kernel(
@@ -947,6 +956,25 @@
     hidden = w_up.shape[2]
     half = count // 2
     parity = jnp.stack([z & 1])
+    if count == BLOCKS:
+        late = call(
+            pack_kernel,
+            shape((PACK, WIDE), BF16),
+            (w_output, jnp.swapaxes(w_up, 1, 2), w_down),
+            scalars=0,
+        )
+    else:
+        late = pad_rows(
+            jnp.concatenate(
+                [
+                    w_output[:, :WIDE],
+                    w_output[:, WIDE:],
+                    jnp.swapaxes(w_up, 1, 2).reshape(GROUPS * hidden, WIDE),
+                    w_down.reshape(GROUPS * hidden, WIDE),
+                ]
+            ),
+            16,
+        )
     lines = [
         to_lines(w_kernel),
         to_lines(w_depth.reshape(-1)),
@@ -962,18 +990,6 @@
             shape((HALF // 2, WIDTH), BF16),
         ),
         (parity, layer_in, w_query, w_key, w_value, w_point, w_convout, small),
-    )
-    early, w_output, w_up, w_down = lax.optimization_barrier((early, w_output, w_up, w_down))
-    late = pad_rows(
-        jnp.concatenate(
-            [
-                w_output[:, :WIDE],
-                w_output[:, WIDE:],
-                jnp.swapaxes(w_up, 1, 2).reshape(GROUPS * hidden, WIDE),
-                w_down.reshape(GROUPS * hidden, WIDE),
-            ]
-        ),
-        16,
     )
     late_all = lax.all_gather(late, ("seq", "dp"), axis=0, tiled=False)
     parts, tokens_a, tokens_b = gather_weights(early, rows, tokens_a, tokens_b)

time: 256 us -> 255 us (level)
  waiting for transfers between devices: 28.4 us -> 20 us
  starting transfers between devices: 62.6 us -> 69.5 us
    all_gather x1, waiting for transfers between devices: 7.06 us -> 0.02 us  [local(): late_all = lax.all_gather(late, ('seq', 'dp'), axis=0, tiled=False)]
    ppermute x32, starting transfers between devices: 47.9 us -> 54.2 us  [swap(): return lax.ppermute(x, axis, [(i, i ^ mask) for i in range(count)])]
    pallas_call x14 -> x15, Pallas kernels: 117 us -> 119 us  [call(): pl.pallas_call(kernel, out_shape=out_shape, in_specs=[smem] * scalars + [...]
  transfers between devices with their start and end apart: 41 -> 41, of which waited for: 11 -> 11; matrix products, arithmetic and copies ran while one was open for 6% -> 7% of each run, Pallas kernels for 31% -> 32%
where the time goes in v1:
time: 255 us; the launch traced here: 251 us
  Pallas kernels  119 us (47%)
  starting transfers between devices  69.5 us (27%)
  local copies, waits for them, and re-layouts  21 us (8%)
  waiting for transfers between devices  20 us (8%)
  between operations  15 us (6%)
  other arithmetic  6.23 us (2%)
    pallas_call x15, Pallas kernels, call(): pl.pallas_call(kernel, out_shape=out_shape, in_specs=[smem] * scalars + [...  119 us
    ppermute x32, starting transfers between devices, swap(): return lax.ppermute(x, axis, [(i, i ^ mask) for i in range(count)])  54.2 us
    ppermute x32, waiting for transfers between devices, swap(): return lax.ppermute(x, axis, [(i, i ^ mask) for i in range(count)])  13.9 us
    ppermute x4, starting transfers between devices, send_pieces(): lax.ppermute(a, ('seq', 'dp'), first)  8.81 us
    unnamed x78, local copies, waits for them, and re-layouts  8.03 us
    ppermute x4, starting transfers between devices, send_pieces(): lax.ppermute(b, ('seq', 'dp'), second)  6.46 us
    ppermute x4, waiting for transfers between devices, send_pieces(): lax.ppermute(b, ('seq', 'dp'), second)  6.1 us
  transfers between devices with their start and end apart: 41, of which 11 were waited for; matrix products, arithmetic and copies ran while one was open for 7% of the time, Pallas kernels for 32%

profile of v1, /device:TPU:0, one launch (start us, length us, event | category | flops | bytes accessed | tf_op | source)
XLA Modules:
  0.0 251.0 jit_solution(9417130095511897951)
XLA Ops:
  7.2 1.6 shard_map.319
  11.8 2.2 shard_map.315
  14.1 5.0 %collective-permute-start.7 = (bf16[128,384]{1,0:T(8,128)(2,1)}, bf16[128,384]{1,0:T(8,128)(2,1)S(1)}, u32[]{:S(2)}, u32[]{:S(2)}) collective-permute-start(bf16[128,384]{1,0:T(8,128)(2,1)} %get-tuple-element.150), channel_id=1, source_target_pairs={{0,24},{8,16},{16,8},{24,0},{1,25},{9,17},{17,9},{25,1},{2,26},{10... | collective-permute-start | bytes 294920 | tf_op jit(solution)/shard_map/ppermute | solution.py:750
  19.7 4.5 %collective-permute-start.1 = (bf16[256,768]{1,0:T(8,128)(2,1)}, bf16[256,768]{1,0:T(8,128)(2,1)}, u32[]{:S(2)}, u32[]{:S(2)}) collective-permute-start(bf16[256,768]{1,0:T(8,128)(2,1)} %get-tuple-element.146), channel_id=1, source_target_pairs={{0,0},{1,8},{2,2},{3,10},{4,4},{5,12},{6,6},{7,14},{8,16},{9,24},{... | collective-permute-start | bytes 1179656 | tf_op jit(solution)/shard_map/ppermute | solution.py:803
  25.1 6.5 %collective-permute-done.6 = bf16[128,384]{1,0:T(8,128)(2,1)S(1)} collective-permute-done((bf16[128,384]{1,0:T(8,128)(2,1)}, bf16[128,384]{1,0:T(8,128)(2,1)S(1)}, u32[]{:S(2)}, u32[]{:S(2)}) %collective-permute-start.6) | collective-permute-done | bytes 98336 | tf_op jit(solution)/shard_map/ppermute | solution.py:750
  32.5 2.6 %collective-permute-start.10 = (bf16[512,384]{1,0:T(8,128)(2,1)S(1)}, bf16[512,384]{1,0:T(8,128)(2,1)S(1)}, u32[]{:S(2)}, u32[]{:S(2)}) collective-permute-start(bf16[512,384]{1,0:T(8,128)(2,1)S(1)} %constant_dynamic-update-slice_fusion.refs_0_), channel_id=1, source_target_pairs={{0,6},{1,7},{2,4},{3,5},{4,2},{5,3},{6,0},{7,1},{8,14},{9,15},{10,... | collective-permute-start | bytes 1179656 | tf_op jit(solution)/shard_map/ppermute | solution.py:750
  36.0 16.6 %collective-permute-start.3 = (bf16[256,768]{1,0:T(8,128)(2,1)}, bf16[256,768]{1,0:T(8,128)(2,1)}, u32[]{:S(2)}, u32[]{:S(2)}) collective-permute-start(bf16[256,768]{1,0:T(8,128)(2,1)} %collective-permute-done.1.own_a), channel_id=1, source_target_pairs={{0,1},{1,0},{2,3},{3,2},{4,5},{5,4},{6,7},{7,6},{8,9},{9,8},{10,11... | collective-permute-start | bytes 1179656 | tf_op jit(solution)/shard_map/ppermute | solution.py:750
  53.3 0.9 collective-permute-done.8.refs_1_
  55.9 1.0 dynamic-slice_bitcast_fusion
  56.8 2.3 collective-permute-start.16
  59.1 4.8 %shard_map.316 = (s32[4]{0:T(128)}, bf16[1024,768]{1,0:T(8,128)(2,1)}, bf16[512,768]{1,0:T(8,128)(2,1)}, bf16[768,768]{1,0:T(8,128)(2,1)}) custom-call(s32[4]{0:T(128)} %pad_add_fusion.place, f32[2,2]{1,0:T(2,128)} %copy-done.26, f32[2,2]{1,0:T(2,128)} %copy-done.27, bf16[256,768]{1,0:T(8,128)(2,1)} %collective-permute-done.1.own_a, ...), custom_call_target="tpu_custom_call" | custom-call | tf_op jit(solution)/shard_map/pallas_call | solution.py:49
  64.0 1.8 collective-permute-start.15
  66.7 13.0 %shard_map.317 = (bf16[1920,384]{1,0:T(8,128)(2,1)}, bf16[1920,384]{1,0:T(8,128)(2,1)}, bf16[256,384]{1,0:T(8,128)(2,1)}, bf16[512,384]{1,0:T(8,128)(2,1)}, bf16...) custom-call(s32[4]{0:T(128)} %get-tuple-element.148.info, ...), custom_call_target="tpu_custom_call" | custom-call | tf_op jit(solution)/shard_map/pallas_call | solution.py:49
  79.7 1.0 slice.353
  80.9 1.1 fusion.60
  84.8 11.5 %shard_map.318 = (bf16[512,768]{1,0:T(8,128)(2,1)}, f32[512,384]{1,0:T(8,128)}, bf16[512,384]{1,0:T(8,128)(2,1)}, bf16[512,768]{1,0:T(8,128)(2,1)}, f32[3,544,128]{2,1,0:T(8,128)}) custom-call(s32[4]{0:T(128)} %get-tuple-element.148.info, bf16[1024,768]{1,0:T(8,128)(2,1)} %get-tuple-element.149.tokens, bf16[1920,384]{1,0:T(8,128)(2,1)} %get-tuple-element.155.own, ...), custom_call_target="tpu_custom_call" | custom-call | tf_op jit(solution)/shard_map/pallas_call | solution.py:49
  97.2 24.1 %shard_map.320 = (bf16[256,768]{1,0:T(8,128)(2,1)}, bf16[256,768]{1,0:T(8,128)(2,1)}, f32[512,768]{1,0:T(8,128)}, bf16[512,768]{1,0:T(8,128)(2,1)}, bf16[16,240,...) custom-call(s32[4]{0:T(128)} %get-tuple-element.148.info, s32[32]{0:T(128)} %copy-done.24, ...), custom_call_target="tpu_custom_call" | custom-call | tf_op jit(solution)/shard_map/pallas_call | solution.py:49
  122.0 13.9 %shard_map.321 = (f32[512,384]{1,0:T(8,128)}, bf16[512,384]{1,0:T(8,128)(2,1)}, f32[384,128]{1,0:T(8,128)}, f32[3,544,128]{2,1,0:T(8,128)}, bf16[16,384]{1,0:T(8,128)(2,1)}) custom-call(s32[4]{0:T(128)} %get-tuple-element.148.info, bf16[512,384]{1,0:T(8,128)(2,1)} %get-tuple-element.157.q, bf16[512,768]{1,0:T(8,128)(2,1)} %get-tuple-element.187.context_grad, ...), custom_call_target="tpu_custom_call" | custom-call | flops 1200000000 | tf_op jit(solution)/shard_map/pallas_call | solution.py:49
  136.0 1.6 copy-done
  137.6 4.6 %shard_map.322 = (bf16[8,112,384]{2,1,0:T(8,128)(2,1)}, bf16[8,112,384]{2,1,0:T(8,128)(2,1)}, bf16[8,128,384]{2,1,0:T(8,128)(2,1)}, bf16[8,128,384]{2,1,0:T(8,128)(2,1)}) custom-call(bf16[16,240,384]{2,1,0:T(8,128)(2,1)} %get-tuple-element.166.kept, bf16[16,240,384]{2,1,0:T(8,128)(2,1)} %copy-done), custom_call_target="tpu_custom_call" | custom-call | tf_op jit(solution)/shard_map/pallas_call | solution.py:49
  142.2 1.6 collective-permute-start.20
  143.9 1.8 collective-permute-start.19
  146.8 1.8 collective-permute-start.18
  148.7 12.5 %shard_map.323 = (f32[512,384]{1,0:T(8,128)}, f32[512,768]{1,0:T(8,128)}, bf16[512,768]{1,0:T(8,128)(2,1)}) custom-call(s32[4]{0:T(128)} %get-tuple-element.148.info, bf16[512,384]{1,0:T(8,128)(2,1)} %get-tuple-element.157.q, bf16[1024,384]{1,0:T(8,128)(2,1)} %get-tuple-element.184.k, bf16[1024,384]{1,0:T(8,128)(2,1)} %get-tuple-element.185.v, ...), custom_call_target="tpu_custom_call" | custom-call | flops 1300000000 | tf_op jit(solution)/shard_map/pallas_call | solution.py:49
  162.3 0.9 fusion.3
  163.2 1.4 collective-permute-start.23
  164.7 2.3 collective-permute-start.24
  167.4 1.6 collective-permute-start.21
  169.5 6.3 %shard_map.324 = (bf16[768,384]{1,0:T(8,128)(2,1)}, f32[16,768]{1,0:T(8,128)}, f32[6,544,128]{2,1,0:T(8,128)}, bf16[16,768]{1,0:T(8,128)(2,1)}) custom-call(s32[4]{0:T(128)} %get-tuple-element.148.info, bf16[1024,768]{1,0:T(8,128)(2,1)} %get-tuple-element.149.tokens, bf16[1920,384]{1,0:T(8,128)(2,1)} %get-tuple-element.155.own, ...), custom_call_target="tpu_custom_call" | custom-call | flops 500000000 | tf_op jit(solution)/shard_map/pallas_call | solution.py:49
  177.8 1.1 fusion.19
  179.1 1.4 collective-permute-done.21.second
  181.5 7.2 %shard_map.325 = (bf16[16,128,384]{2,1,0:T(8,128)(2,1)}, bf16[16,128,384]{2,1,0:T(8,128)(2,1)}, bf16[4,512,384]{2,1,0:T(8,128)(2,1)}) custom-call(s32[4]{0:T(128)} %get-tuple-element.148.info, bf16[1024,768]{1,0:T(8,128)(2,1)} %get-tuple-element.149.tokens, f32[512,384]{1,0:T(8,128)} %get-tuple-element.212.query_attn, ...), custom_call_target="tpu_custom_call" | custom-call | flops 800000000 | tf_op jit(solution)/shard_map/pallas_call | solution.py:49
  188.9 2.2 collective-permute-start.31
  191.1 2.0 collective-permute-start.32
  193.1 1.2 collective-permute-done.27.rim_inputs
  194.3 1.1 copy-done.1
  195.4 3.2 %shard_map.326 = (bf16[8,64,384]{2,1,0:T(8,128)(2,1)}, bf16[8,64,384]{2,1,0:T(8,128)(2,1)}, bf16[8,64,384]{2,1,0:T(8,128)(2,1)}, bf16[8,64,384]{2,1,0:T(8,128)(2,1)}) custom-call(bf16[16,128,384]{2,1,0:T(8,128)(2,1)} %get-tuple-element.222.kept, bf16[16,128,384]{2,1,0:T(8,128)(2,1)} %copy-done.1), custom_call_target="tpu_custom_call" | custom-call | tf_op jit(solution)/shard_map/pallas_call | solution.py:49
  199.7 9.3 %shard_map.327 = (bf16[256,768]{1,0:T(8,128)(2,1)}, bf16[256,768]{1,0:T(8,128)(2,1)}) custom-call(s32[4]{0:T(128)} %get-tuple-element.148.info, bf16[1920,384]{1,0:T(8,128)(2,1)} %get-tuple-element.155.own, bf16[1920,384]{1,0:T(8,128)(2,1)} %get-tuple-element.156.other, bf16[768,768]{1,0:T(8,128)(2,1)} %get-tuple-element.163.matrix, ...), custom_call_target="tpu_custom_call" | custom-call | flops 800000000 | tf_op jit(solution)/shard_map/pallas_call | solution.py:49
  212.0 1.1 collective-permute-start.33
  213.0 1.5 collective-permute-start.34
  214.5 2.5 %collective-permute-start.36 = (bf16[256,768]{1,0:T(8,128)(2,1)S(1)}, bf16[256,768]{1,0:T(8,128)(2,1)S(1)}, u32[]{:S(2)}, u32[]{:S(2)}) collective-permute-start(bf16[256,768]{1,0:T(8,128)(2,1)S(1)} %copy-done.31), channel_id=1, source_target_pairs={{16,0},{24,1},{18,2},{26,3},{20,4},{28,5},{22,6},{30,7},{0,8},{8,9... | collective-permute-start | bytes 1179656 | tf_op jit(solution)/shard_map/ppermute | solution.py:803
  217.0 2.4 collective-permute-done.33
  219.4 1.0 collective-permute-done.34
  220.6 7.8 %collective-permute-start.37 = (bf16[128,384]{1,0:T(8,128)(2,1)S(1)}, bf16[128,384]{1,0:T(8,128)(2,1)S(1)}, u32[]{:S(2)}, u32[]{:S(2)}) collective-permute-start(bf16[128,384]{1,0:T(8,128)(2,1)S(1)} %pad_maximum_fusion.6), channel_id=1, source_target_pairs={{0,8},{8,0},{16,24},{24,16},{1,9},{9,1},{17,25},{25,17},{2,10},{10... | collective-permute-start | bytes 294920 | tf_op jit(solution)/shard_map/ppermute | solution.py:750
  228.4 2.4 collective-permute-start.39
  231.5 2.0 shard_map.328
  233.5 4.7 %collective-permute-done.36.second = bf16[256,768]{1,0:T(8,128)(2,1)S(1)} collective-permute-done((bf16[256,768]{1,0:T(8,128)(2,1)S(1)}, bf16[256,768]{1,0:T(8,128)(2,1)S(1)}, u32[]{:S(2)}, u32[]{:S(2)}) %collective-permute-start.36) | collective-permute-done | bytes 393248 | tf_op jit(solution)/shard_map/ppermute | solution.py:803
  238.9 2.4 shard_map.329
  (204 shorter events, 28.3 us)
Async XLA Ops:
  7.2 89.2 %all-gather.3.cloned.1.call-start = ((), (), s32[]{:S(2)}) async-start(), calls=%async_computation | async-start | bytes 6082560 | tf_op jit(solution)/shard_map/all_gather | solution.py:994
  11.8 40.9 %copy-start.28 = (s32[2,1]{0,1:T(1,128)S(1)}, s32[2,1]{0,1:T(1,128)}, u32[]{:S(2)}) copy-start(s32[2,1]{0,1:T(1,128)} %param.23) | copy-start | bytes 28
  11.8 40.9 %copy-start.29 = (s32[2,1]{0,1:T(1,128)S(1)}, s32[2,1]{0,1:T(1,128)}, u32[]{:S(2)}) copy-start(s32[2,1]{0,1:T(1,128)} %param.22) | copy-start | bytes 28
  11.8 44.0 %copy-start.35 = (s32[32]{0:T(128)S(1)}, s32[32]{0:T(128)}, u32[]{:S(2)}) copy-start(s32[32]{0:T(128)} %constant.34.clone) | copy-start | bytes 388
  11.8 44.0 %copy-start.3 = (bf16[2,1,256,768]{3,2,1,0:T(8,128)(2,1)S(1)}, bf16[2,1,256,768]{3,2,1,0:T(8,128)(2,1)}, u32[]{:S(2)}) copy-start(bf16[2,1,256,768]{3,2,1,0:T(8,128)(2,1)} %param.21) | copy-start | bytes 2359300
  14.1 11.0 %collective-permute-start.7 = (bf16[128,384]{1,0:T(8,128)(2,1)}, bf16[128,384]{1,0:T(8,128)(2,1)S(1)}, u32[]{:S(2)}, u32[]{:S(2)}) collective-permute-start(bf16[128,384]{1,0:T(8,128)(2,1)} %get-tuple-element.150), channel_id=1, source_target_pairs={{0,24},{8,16},{16,8},{24,0},{1,25},{9,17},{17,9},{25,1},{2,26},{10... | collective-permute-start | bytes 294920 | tf_op jit(solution)/shard_map/ppermute | solution.py:750
  19.1 12.5 %collective-permute-start.6 = (bf16[128,384]{1,0:T(8,128)(2,1)}, bf16[128,384]{1,0:T(8,128)(2,1)S(1)}, u32[]{:S(2)}, u32[]{:S(2)}) collective-permute-start(bf16[128,384]{1,0:T(8,128)(2,1)} %get-tuple-element.150), channel_id=1, source_target_pairs={{0,16},{8,24},{16,0},{24,8},{1,17},{9,25},{17,1},{25,9},{2,18},{10... | collective-permute-start | bytes 294920 | tf_op jit(solution)/shard_map/ppermute | solution.py:750
  19.1 12.5 %collective-permute-start.5 = (bf16[128,384]{1,0:T(8,128)(2,1)}, bf16[128,384]{1,0:T(8,128)(2,1)S(1)}, u32[]{:S(2)}, u32[]{:S(2)}) collective-permute-start(bf16[128,384]{1,0:T(8,128)(2,1)} %get-tuple-element.150), channel_id=1, source_target_pairs={{0,8},{8,0},{16,24},{24,16},{1,9},{9,1},{17,25},{25,17},{2,10},{10... | collective-permute-start | bytes 294920 | tf_op jit(solution)/shard_map/ppermute | solution.py:750
  19.7 16.4 %collective-permute-start.1 = (bf16[256,768]{1,0:T(8,128)(2,1)}, bf16[256,768]{1,0:T(8,128)(2,1)}, u32[]{:S(2)}, u32[]{:S(2)}) collective-permute-start(bf16[256,768]{1,0:T(8,128)(2,1)} %get-tuple-element.146), channel_id=1, source_target_pairs={{0,0},{1,8},{2,2},{3,10},{4,4},{5,12},{6,6},{7,14},{8,16},{9,24},{... | collective-permute-start | bytes 1179656 | tf_op jit(solution)/shard_map/ppermute | solution.py:803
  24.2 28.5 %collective-permute-start.2 = (bf16[256,768]{1,0:T(8,128)(2,1)}, bf16[256,768]{1,0:T(8,128)(2,1)}, u32[]{:S(2)}, u32[]{:S(2)}) collective-permute-start(bf16[256,768]{1,0:T(8,128)(2,1)} %get-tuple-element.147), channel_id=1, source_target_pairs={{0,16},{1,24},{2,18},{3,26},{4,20},{5,28},{6,22},{7,30},{8,0},{9,8... | collective-permute-start | bytes 1179656 | tf_op jit(solution)/shard_map/ppermute | solution.py:803
  32.5 31.5 %copy-start.2 = (bf16[512,384]{1,0:T(8,128)(2,1)}, bf16[512,384]{1,0:T(8,128)(2,1)S(1)}, u32[]{:S(2)}) copy-start(bf16[512,384]{1,0:T(8,128)(2,1)S(1)} %constant_dynamic-update-slice_fusion.refs_0_) | copy-start | bytes 1179652
  32.5 20.3 %collective-permute-start.10 = (bf16[512,384]{1,0:T(8,128)(2,1)S(1)}, bf16[512,384]{1,0:T(8,128)(2,1)S(1)}, u32[]{:S(2)}, u32[]{:S(2)}) collective-permute-start(bf16[512,384]{1,0:T(8,128)(2,1)S(1)} %constant_dynamic-update-slice_fusion.refs_0_), channel_id=1, source_target_pairs={{0,6},{1,7},{2,4},{3,5},{4,2},{5,3},{6,0},{7,1},{8,14},{9,15},{10,... | collective-permute-start | bytes 1179656 | tf_op jit(solution)/shard_map/ppermute | solution.py:750
  35.1 18.2 %collective-permute-start.9 = (bf16[512,384]{1,0:T(8,128)(2,1)S(1)}, bf16[512,384]{1,0:T(8,128)(2,1)S(1)}, u32[]{:S(2)}, u32[]{:S(2)}) collective-permute-start(bf16[512,384]{1,0:T(8,128)(2,1)S(1)} %constant_dynamic-update-slice_fusion.refs_0_), channel_id=1, source_target_pairs={{0,4},{1,5},{2,6},{3,7},{4,0},{5,1},{6,2},{7,3},{8,12},{9,13},{10,... | collective-permute-start | bytes 1179656 | tf_op jit(solution)/shard_map/ppermute | solution.py:750
  35.5 18.7 %collective-permute-start.8 = (bf16[512,384]{1,0:T(8,128)(2,1)S(1)}, bf16[512,384]{1,0:T(8,128)(2,1)S(1)}, u32[]{:S(2)}, u32[]{:S(2)}) collective-permute-start(bf16[512,384]{1,0:T(8,128)(2,1)S(1)} %constant_dynamic-update-slice_fusion.refs_0_), channel_id=1, source_target_pairs={{0,2},{1,3},{2,0},{3,1},{4,6},{5,7},{6,4},{7,5},{8,10},{9,11},{10,... | collective-permute-start | bytes 1179656 | tf_op jit(solution)/shard_map/ppermute | solution.py:750
  36.0 18.8 %collective-permute-start.3 = (bf16[256,768]{1,0:T(8,128)(2,1)}, bf16[256,768]{1,0:T(8,128)(2,1)}, u32[]{:S(2)}, u32[]{:S(2)}) collective-permute-start(bf16[256,768]{1,0:T(8,128)(2,1)} %collective-permute-done.1.own_a), channel_id=1, source_target_pairs={{0,1},{1,0},{2,3},{3,2},{4,5},{5,4},{6,7},{7,6},{8,9},{9,8},{10,11... | collective-permute-start | bytes 1179656 | tf_op jit(solution)/shard_map/ppermute | solution.py:750
  52.7 2.0 collective-permute-start
  52.8 4.0 %collective-permute-start.4 = (bf16[256,768]{1,0:T(8,128)(2,1)}, bf16[256,768]{1,0:T(8,128)(2,1)}, u32[]{:S(2)}, u32[]{:S(2)}) collective-permute-start(bf16[256,768]{1,0:T(8,128)(2,1)} %collective-permute-done.2.own_b), channel_id=1, source_target_pairs={{0,1},{1,0},{2,3},{3,2},{4,5},{5,4},{6,7},{7,6},{8,9},{9,8},{10,11... | collective-permute-start | bytes 1179656 | tf_op jit(solution)/shard_map/ppermute | solution.py:750
  54.2 9.8 %collective-permute-start.11 = (bf16[512,384]{1,0:T(8,128)(2,1)S(1)}, bf16[512,384]{1,0:T(8,128)(2,1)S(1)}, u32[]{:S(2)}, u32[]{:S(2)}) collective-permute-start(bf16[512,384]{1,0:T(8,128)(2,1)S(1)} %constant_dynamic-update-slice_fusion.refs_0_), channel_id=1, source_target_pairs={{0,1},{1,0},{2,3},{3,2},{4,5},{5,4},{6,7},{7,6},{8,9},{9,8},{10,11... | collective-permute-start | bytes 1179656 | tf_op jit(solution)/shard_map/ppermute | solution.py:750
  54.2 11.6 %collective-permute-start.12 = (bf16[512,384]{1,0:T(8,128)(2,1)S(1)}, bf16[512,384]{1,0:T(8,128)(2,1)S(1)}, u32[]{:S(2)}, u32[]{:S(2)}) collective-permute-start(bf16[512,384]{1,0:T(8,128)(2,1)S(1)} %collective-permute-done.8.refs_1_), channel_id=1, source_target_pairs={{0,1},{1,0},{2,3},{3,2},{4,5},{5,4},{6,7},{7,6},{8,9},{9,8},{10,11... | collective-permute-start | bytes 1179656 | tf_op jit(solution)/shard_map/ppermute | solution.py:750
  54.7 11.1 %collective-permute-start.13 = (bf16[512,384]{1,0:T(8,128)(2,1)S(1)}, bf16[512,384]{1,0:T(8,128)(2,1)S(1)}, u32[]{:S(2)}, u32[]{:S(2)}) collective-permute-start(bf16[512,384]{1,0:T(8,128)(2,1)S(1)} %collective-permute-done.9.refs_2_), channel_id=1, source_target_pairs={{0,1},{1,0},{2,3},{3,2},{4,5},{5,4},{6,7},{7,6},{8,9},{9,8},{10,11... | collective-permute-start | bytes 1179656 | tf_op jit(solution)/shard_map/ppermute | solution.py:750
  54.8 11.0 %collective-permute-start.14 = (bf16[512,384]{1,0:T(8,128)(2,1)S(1)}, bf16[512,384]{1,0:T(8,128)(2,1)}, u32[]{:S(2)}, u32[]{:S(2)}) collective-permute-start(bf16[512,384]{1,0:T(8,128)(2,1)S(1)} %collective-permute-done.10.refs_3_), channel_id=1, source_target_pairs={{0,1},{1,0},{2,3},{3,2},{4,5},{5,4},{6,7},{7,6},{8,9},{9,8},{10,11... | collective-permute-start | bytes 1179656 | tf_op jit(solution)/shard_map/ppermute | solution.py:750
  55.9 27.4 %copy-start.24 = (s32[32]{0:T(128)}, s32[32]{0:T(128)S(1)}, u32[]{:S(2)}) copy-start(s32[32]{0:T(128)S(1)} %broadcast_xor_fusion.order) | copy-start | bytes 388
  56.8 39.5 %collective-permute-start.16 = (bf16[256,768]{1,0:T(8,128)(2,1)}, bf16[256,768]{1,0:T(8,128)(2,1)S(1)}, u32[]{:S(2)}, u32[]{:S(2)}) collective-permute-start(bf16[256,768]{1,0:T(8,128)(2,1)} %get-tuple-element.288), channel_id=1, source_target_pairs={{0,16},{1,24},{2,18},{3,26},{4,20},{5,28},{6,22},{7,30},{8,0},{9,8... | collective-permute-start | bytes 1179656 | tf_op jit(solution)/shard_map/ppermute | solution.py:803
  64.0 32.4 %collective-permute-start.15 = (bf16[256,768]{1,0:T(8,128)(2,1)}, bf16[256,768]{1,0:T(8,128)(2,1)S(1)}, u32[]{:S(2)}, u32[]{:S(2)}) collective-permute-start(bf16[256,768]{1,0:T(8,128)(2,1)} %get-tuple-element.289), channel_id=1, source_target_pairs={{0,0},{1,8},{2,2},{3,10},{4,4},{5,12},{6,6},{7,14},{8,16},{9,24},{... | collective-permute-start | bytes 1179656 | tf_op jit(solution)/shard_map/ppermute | solution.py:803
  121.3 14.7 %collective-permute-start.17 = (bf16[16,240,384]{2,1,0:T(8,128)(2,1)}, bf16[16,240,384]{2,1,0:T(8,128)(2,1)S(1)}, u32[]{:S(2)}, u32[]{:S(2)}) collective-permute-start(bf16[16,240,384]{2,1,0:T(8,128)(2,1)} %get-tuple-element.167), channel_id=1, source_target_pairs={{0,1},{1,0},{2,3},{3,2},{4,5},{5,4},{6,7},{7,6},{8,9},{9,8},{10,11... | collective-permute-start | bytes 8847368 | tf_op jit(solution)/shard_map/ppermute | solution.py:750
  142.2 19.7 %collective-permute-start.20 = (bf16[2,4,128,384]{3,2,1,0:T(8,128)(2,1)}, bf16[2,4,128,384]{3,2,1,0:T(8,128)(2,1)S(1)}, u32[]{:S(2)}, u32[]{:S(2)}) collective-permute-start(bf16[2,4,128,384]{3,2,1,0:T(8,128)(2,1)} %bitcast.123), channel_id=1, source_target_pairs={{0,2},{1,3},{2,0},{3,1},{4,6},{5,7},{6,4},{7,5},{8,10},{9,11},{10,... | collective-permute-start | bytes 2359304 | tf_op jit(solution)/shard_map/ppermute | solution.py:750
  143.9 17.9 %collective-permute-start.19 = (bf16[2,4,112,384]{3,2,1,0:T(8,128)(2,1)}, bf16[2,4,112,384]{3,2,1,0:T(8,128)(2,1)S(1)}, u32[]{:S(2)}, u32[]{:S(2)}) collective-permute-start(bf16[2,4,112,384]{3,2,1,0:T(8,128)(2,1)} %bitcast.124), channel_id=1, source_target_pairs={{0,4},{1,5},{2,6},{3,7},{4,0},{5,1},{6,2},{7,3},{8,12},{9,13},{10,... | collective-permute-start | bytes 2064392 | tf_op jit(solution)/shard_map/ppermute | solution.py:750
  146.8 22.2 %collective-permute-start.18 = (bf16[256,768]{1,0:T(8,128)(2,1)}, bf16[256,768]{1,0:T(8,128)(2,1)S(1)}, u32[]{:S(2)}, u32[]{:S(2)}) collective-permute-start(bf16[256,768]{1,0:T(8,128)(2,1)} %get-tuple-element.180), channel_id=1, source_target_pairs={{0,0},{8,1},{2,2},{10,3},{4,4},{12,5},{6,6},{14,7},{16,8},{24,9},{... | collective-permute-start | bytes 1179656 | tf_op jit(solution)/shard_map/ppermute | solution.py:803
  163.2 14.5 %collective-permute-start.23 = (bf16[4,112,384]{2,1,0:T(8,128)(2,1)}, bf16[4,112,384]{2,1,0:T(8,128)(2,1)}, u32[]{:S(2)}, u32[]{:S(2)}) collective-permute-start(bf16[4,112,384]{2,1,0:T(8,128)(2,1)} %get-tuple-element.199), channel_id=1, source_target_pairs={{0,2},{1,3},{2,0},{3,1},{4,6},{5,7},{6,4},{7,5},{8,10},{9,11},{10,... | collective-permute-start | bytes 1032200 | tf_op jit(solution)/shard_map/ppermute | solution.py:750
  164.7 13.1 %collective-permute-start.24 = (bf16[4,128,384]{2,1,0:T(8,128)(2,1)S(1)}, bf16[4,128,384]{2,1,0:T(8,128)(2,1)S(1)}, u32[]{:S(2)}, u32[]{:S(2)}) collective-permute-start(bf16[4,128,384]{2,1,0:T(8,128)(2,1)S(1)} %get-tuple-element.200), channel_id=1, source_target_pairs={{0,4},{1,5},{2,6},{3,7},{4,0},{5,1},{6,2},{7,3},{8,12},{9,13},{10,... | collective-permute-start | bytes 1179656 | tf_op jit(solution)/shard_map/ppermute | solution.py:750
  167.3 11.8 %collective-permute-start.22 = (bf16[16,384]{1,0:T(8,128)(2,1)S(1)}, bf16[16,384]{1,0:T(8,128)(2,1)S(1)}, u32[]{:S(2)}, u32[]{:S(2)}) collective-permute-start(bf16[16,384]{1,0:T(8,128)(2,1)S(1)} %copy-done.34), channel_id=1, source_target_pairs={{0,1},{1,0},{2,3},{3,2},{4,5},{5,4},{6,7},{7,6},{8,9},{9,8},{10,11... | collective-permute-start | bytes 36872 | tf_op jit(solution)/shard_map/ppermute | solution.py:750
  167.4 13.2 %collective-permute-start.21 = (bf16[256,768]{1,0:T(8,128)(2,1)S(1)}, bf16[256,768]{1,0:T(8,128)(2,1)S(1)}, u32[]{:S(2)}, u32[]{:S(2)}) collective-permute-start(bf16[256,768]{1,0:T(8,128)(2,1)S(1)} %copy-done.30), channel_id=1, source_target_pairs={{16,0},{24,1},{18,2},{26,3},{20,4},{28,5},{22,6},{30,7},{0,8},{8,9... | collective-permute-start | bytes 1179656 | tf_op jit(solution)/shard_map/ppermute | solution.py:803
  169.0 11.6 %collective-permute-start.25 = (bf16[512,768]{1,0:T(8,128)(2,1)}, bf16[512,768]{1,0:T(8,128)(2,1)S(1)}, u32[]{:S(2)}, u32[]{:S(2)}) collective-permute-start(bf16[512,768]{1,0:T(8,128)(2,1)} %get-tuple-element.215), channel_id=1, source_target_pairs={{0,1},{1,0},{2,3},{3,2},{4,5},{5,4},{6,7},{7,6},{8,9},{9,8},{10,11... | collective-permute-start | bytes 2359304 | tf_op jit(solution)/shard_map/ppermute | solution.py:750
  180.6 18.1 %copy-start.18 = (bf16[256,768]{1,0:T(8,128)(2,1)}, bf16[256,768]{1,0:T(8,128)(2,1)S(1)}, u32[]{:S(2)}) copy-start(bf16[256,768]{1,0:T(8,128)(2,1)S(1)} %collective-permute-done.21.second) | copy-start | bytes 1179652
  188.7 5.6 %collective-permute-start.26 = (bf16[16,128,384]{2,1,0:T(8,128)(2,1)}, bf16[16,128,384]{2,1,0:T(8,128)(2,1)S(1)}, u32[]{:S(2)}, u32[]{:S(2)}) collective-permute-start(bf16[16,128,384]{2,1,0:T(8,128)(2,1)} %get-tuple-element.223), channel_id=1, source_target_pairs={{0,1},{1,0},{2,3},{3,2},{4,5},{5,4},{6,7},{7,6},{8,9},{9,8},{10,11... | collective-permute-start | bytes 4718600 | tf_op jit(solution)/shard_map/ppermute | solution.py:750
  188.7 20.3 %collective-permute-start.30 = (bf16[240,384]{1,0:T(8,128)(2,1)S(1)}, bf16[240,384]{1,0:T(8,128)(2,1)S(1)}, u32[]{:S(2)}, u32[]{:S(2)}) collective-permute-start(bf16[240,384]{1,0:T(8,128)(2,1)S(1)} %pad_maximum_fusion.2), channel_id=1, source_target_pairs={{0,8},{8,0},{16,24},{24,16},{1,9},{9,1},{17,25},{25,17},{2,10},{10... | collective-permute-start | bytes 552968 | tf_op jit(solution)/shard_map/ppermute | solution.py:750
  188.9 20.1 %collective-permute-start.31 = (bf16[240,384]{1,0:T(8,128)(2,1)S(1)}, bf16[240,384]{1,0:T(8,128)(2,1)S(1)}, u32[]{:S(2)}, u32[]{:S(2)}) collective-permute-start(bf16[240,384]{1,0:T(8,128)(2,1)S(1)} %pad_maximum_fusion.3), channel_id=1, source_target_pairs={{0,16},{8,24},{16,0},{24,8},{1,17},{9,25},{17,1},{25,9},{2,18},{10... | collective-permute-start | bytes 552968 | tf_op jit(solution)/shard_map/ppermute | solution.py:750
  191.1 17.9 %collective-permute-start.32 = (bf16[240,384]{1,0:T(8,128)(2,1)S(1)}, bf16[240,384]{1,0:T(8,128)(2,1)S(1)}, u32[]{:S(2)}, u32[]{:S(2)}) collective-permute-start(bf16[240,384]{1,0:T(8,128)(2,1)S(1)} %pad_maximum_fusion.4), channel_id=1, source_target_pairs={{0,24},{8,16},{16,8},{24,0},{1,25},{9,17},{17,9},{25,1},{2,26},{10... | collective-permute-start | bytes 552968 | tf_op jit(solution)/shard_map/ppermute | solution.py:750
  193.1 1.2 collective-permute-start.27
  198.6 11.4 %collective-permute-start.28 = (bf16[2,4,64,384]{3,2,1,0:T(8,128)(2,1)}, bf16[2,4,64,384]{3,2,1,0:T(8,128)(2,1)S(1)}, u32[]{:S(2)}, u32[]{:S(2)}) collective-permute-start(bf16[2,4,64,384]{3,2,1,0:T(8,128)(2,1)} %bitcast.126), channel_id=1, source_target_pairs={{0,4},{1,5},{2,6},{3,7},{4,0},{5,1},{6,2},{7,3},{8,12},{9,13},{10,... | collective-permute-start | bytes 1179656 | tf_op jit(solution)/shard_map/ppermute | solution.py:750
  199.2 11.1 %collective-permute-start.29 = (bf16[2,4,64,384]{3,2,1,0:T(8,128)(2,1)}, bf16[2,4,64,384]{3,2,1,0:T(8,128)(2,1)S(1)}, u32[]{:S(2)}, u32[]{:S(2)}) collective-permute-start(bf16[2,4,64,384]{3,2,1,0:T(8,128)(2,1)} %bitcast.125), channel_id=1, source_target_pairs={{0,2},{1,3},{2,0},{3,1},{4,6},{5,7},{6,4},{7,5},{8,10},{9,11},{10,... | collective-permute-start | bytes 1179656 | tf_op jit(solution)/shard_map/ppermute | solution.py:750
  210.5 9.9 %collective-permute-start.35 = (bf16[256,768]{1,0:T(8,128)(2,1)S(1)}, bf16[256,768]{1,0:T(8,128)(2,1)S(1)}, u32[]{:S(2)}, u32[]{:S(2)}) collective-permute-start(bf16[256,768]{1,0:T(8,128)(2,1)S(1)} %copy-done.32), channel_id=1, source_target_pairs={{0,0},{8,1},{2,2},{10,3},{4,4},{12,5},{6,6},{14,7},{16,8},{24,9},{... | collective-permute-start | bytes 1179656 | tf_op jit(solution)/shard_map/ppermute | solution.py:803
  212.0 7.4 %collective-permute-start.33 = (bf16[4,64,384]{2,1,0:T(8,128)(2,1)S(1)}, bf16[4,64,384]{2,1,0:T(8,128)(2,1)S(1)}, u32[]{:S(2)}, u32[]{:S(2)}) collective-permute-start(bf16[4,64,384]{2,1,0:T(8,128)(2,1)S(1)} %get-tuple-element.253), channel_id=1, source_target_pairs={{0,2},{1,3},{2,0},{3,1},{4,6},{5,7},{6,4},{7,5},{8,10},{9,11},{10,... | collective-permute-start | bytes 589832 | tf_op jit(solution)/shard_map/ppermute | solution.py:750
  213.0 7.4 %collective-permute-start.34 = (bf16[4,64,384]{2,1,0:T(8,128)(2,1)S(1)}, bf16[4,64,384]{2,1,0:T(8,128)(2,1)S(1)}, u32[]{:S(2)}, u32[]{:S(2)}) collective-permute-start(bf16[4,64,384]{2,1,0:T(8,128)(2,1)S(1)} %get-tuple-element.254), channel_id=1, source_target_pairs={{0,4},{1,5},{2,6},{3,7},{4,0},{5,1},{6,2},{7,3},{8,12},{9,13},{10,... | collective-permute-start | bytes 589832 | tf_op jit(solution)/shard_map/ppermute | solution.py:750
  214.5 23.7 %collective-permute-start.36 = (bf16[256,768]{1,0:T(8,128)(2,1)S(1)}, bf16[256,768]{1,0:T(8,128)(2,1)S(1)}, u32[]{:S(2)}, u32[]{:S(2)}) collective-permute-start(bf16[256,768]{1,0:T(8,128)(2,1)S(1)} %copy-done.31), channel_id=1, source_target_pairs={{16,0},{24,1},{18,2},{26,3},{20,4},{28,5},{22,6},{30,7},{0,8},{8,9... | collective-permute-start | bytes 1179656 | tf_op jit(solution)/shard_map/ppermute | solution.py:803
  220.6 20.7 %collective-permute-start.37 = (bf16[128,384]{1,0:T(8,128)(2,1)S(1)}, bf16[128,384]{1,0:T(8,128)(2,1)S(1)}, u32[]{:S(2)}, u32[]{:S(2)}) collective-permute-start(bf16[128,384]{1,0:T(8,128)(2,1)S(1)} %pad_maximum_fusion.6), channel_id=1, source_target_pairs={{0,8},{8,0},{16,24},{24,16},{1,9},{9,1},{17,25},{25,17},{2,10},{10... | collective-permute-start | bytes 294920 | tf_op jit(solution)/shard_map/ppermute | solution.py:750
  228.4 12.9 %collective-permute-start.38 = (bf16[128,384]{1,0:T(8,128)(2,1)S(1)}, bf16[128,384]{1,0:T(8,128)(2,1)S(1)}, u32[]{:S(2)}, u32[]{:S(2)}) collective-permute-start(bf16[128,384]{1,0:T(8,128)(2,1)S(1)} %pad_maximum_fusion.7), channel_id=1, source_target_pairs={{0,16},{8,24},{16,0},{24,8},{1,17},{9,25},{17,1},{25,9},{2,18},{10... | collective-permute-start | bytes 294920 | tf_op jit(solution)/shard_map/ppermute | solution.py:750
  228.4 12.9 %collective-permute-start.39 = (bf16[128,384]{1,0:T(8,128)(2,1)S(1)}, bf16[128,384]{1,0:T(8,128)(2,1)S(1)}, u32[]{:S(2)}, u32[]{:S(2)}) collective-permute-start(bf16[128,384]{1,0:T(8,128)(2,1)S(1)} %pad_maximum_fusion.8), channel_id=1, source_target_pairs={{0,24},{8,16},{16,8},{24,0},{1,25},{9,17},{17,9},{25,1},{2,26},{10... | collective-permute-start | bytes 294920 | tf_op jit(solution)/shard_map/ppermute | solution.py:750
  (29 other events, 147.3 us)
Sparse Core Ops, SparseCore 0:
  10.9 83.8 all-gather.2
